TPU v7x, 32 devices: a whole 2x2x4 slice. The times are simulated.
32 devices in a mesh: wide: 16 (over z, y, core), narrow: 2 (over x).
Axes of the slice: x: 2, y: 2, z: 4, core: 2. Of those that a mesh axis runs over, the one named last changes fastest.
Arguments:
- pixels: bfloat16 [2, 32, 272, 261], P(None, ('wide', 'narrow')), may hold values from -4 to 4
- labels: int32 [2, 32], P(None, ('wide', 'narrow')), may hold values from 0 to 999
- partner: int32 [2, 32], P(None, ('wide', 'narrow')), may hold values from 0 to 31
- pair_on: int32 [2, 32], P(None, ('wide', 'narrow')), may hold values 0 or 1
- step_count: int32 [1], replicated, may hold values from 1 to 20
- matrices: float32 [1024, 10240], P(('wide', 'narrow')), may hold values from -0.75 to 0.75, as said below
- kv_weight: float32 [2048, 261], P(('wide', 'narrow')), may hold values from -0.375 to 0.375
- norm_gains: float32 [1024, 10], P(('wide', 'narrow')), may hold values from -1.2 to 1.4, as said below
- head_weight: float32 [1024, 1000], P(('wide', 'narrow')), may hold values from -0.1875 to 0.1875
- latent_init: float32 [1024, 512], P(('wide', 'narrow')), may hold values from -5 to 5
- matrices_first: float32 [1024, 10240], P(('wide', 'narrow')), may hold values from -3.8146973e-05 to 3.8146973e-05
- kv_first: float32 [2048, 261], P(('wide', 'narrow')), may hold values from -3.8146973e-05 to 3.8146973e-05
- gains_first: float32 [1024, 10], P(('wide', 'narrow')), may hold values from -3.8146973e-05 to 3.8146973e-05
- head_first: float32 [1024, 1000], P(('wide', 'narrow')), may hold values from -3.8146973e-05 to 3.8146973e-05
- latent_first: float32 [1024, 512], P(('wide', 'narrow')), may hold values from -8.34465e-07 to 8.34465e-07
- matrices_second: float32 [1024, 10240], P(('wide', 'narrow')), may hold values from 7.949873e-12 to 3.1799494e-11
- kv_second: float32 [2048, 261], P(('wide', 'narrow')), may hold values from 7.949873e-12 to 3.1799494e-11
- gains_second: float32 [1024, 10], P(('wide', 'narrow')), may hold values from 7.949873e-12 to 3.1799494e-11
- head_second: float32 [1024, 1000], P(('wide', 'narrow')), may hold values from 7.949873e-12 to 3.1799494e-11
- latent_second: float32 [1024, 512], P(('wide', 'narrow')), may hold values from 1.5899748e-15 to 6.359899e-15
Outputs:
- total_loss: float32 [], replicated
- grad_norm: float32 [], replicated
- counts: int32 [2], replicated
- new_matrices_first: float32 [1024, 10240], P(('wide', 'narrow'))
- new_matrices_second: float32 [1024, 10240], P(('wide', 'narrow'))
- new_matrices: float32 [1024, 10240], P(('wide', 'narrow'))
- new_kv_first: float32 [2048, 261], P(('wide', 'narrow'))
- new_kv_second: float32 [2048, 261], P(('wide', 'narrow'))
- new_kv_weight: float32 [2048, 261], P(('wide', 'narrow'))
- new_gains_first: float32 [1024, 10], P(('wide', 'narrow'))
- new_gains_second: float32 [1024, 10], P(('wide', 'narrow'))
- clipped_gains: float32 [1024, 10], P(('wide', 'narrow'))
- new_head_first: float32 [1024, 1000], P(('wide', 'narrow'))
- new_head_second: float32 [1024, 1000], P(('wide', 'narrow'))
- new_head_weight: float32 [1024, 1000], P(('wide', 'narrow'))
- new_latent_first: float32 [1024, 512], P(('wide', 'narrow'))
- new_latent_second: float32 [1024, 512], P(('wide', 'narrow'))
- clipped_latent: float32 [1024, 512], P(('wide', 'narrow'))
Inputs may be any that keep to these rules, and one draw needn't show every extreme that they name: `matrices`: the cross and latent output blocks (1 and 7) are four times larger than the others. `norm_gains`: even columns are gains, odd columns biases.
All inputs are finite; a program needn't handle non-finite values. No bound on the sum of `pair_on` on one device may be relied on, other than what follows from the above.
Results may differ from a plain program's by a relative error of at most 0.012.
The roundings to bfloat16 on the way count: a program that leaves them out, or rounds other values in their place, can miss the bound.
Values may be sent and summed in bfloat16 or wider, within the bound.
No kernel may reach another device: no remote copies, remote signals or barrier semaphores. Data moves between devices by JAX's collectives and lax.ppermute only.
A program may use at most 320 MiB of HBM per device.

v0:
```python
import jax
import jax.numpy as jnp
from jax import lax
from jax.sharding import PartitionSpec as P

HEADS = 8
REPEATS = 1


EPSILON = 1e-05
RATE = 0.03
DECAY = 0.1
TINY = 1e-08
THRESH = 0.01


def lowered(values):
    return values.astype(jnp.bfloat16)


def matmul(first_op, second_op):
    return jnp.dot(first_op, second_op, preferred_element_type=jnp.float32)


def left_dot(first_op, second_op):
    return lax.dot_general(
        first_op, second_op, (((0,), (0,)), ((), ())), preferred_element_type=jnp.float32
    )


def right_dot(first_op, second_op):
    return lax.dot_general(
        first_op, second_op, (((1,), (1,)), ((), ())), preferred_element_type=jnp.float32
    )


def layer_norm(inputs, gain_vec, bias_vec):
    center = inputs - jnp.mean(inputs, axis=-1, keepdims=True)
    spread = jnp.mean(center * center, axis=-1, keepdims=True)
    return center * lax.rsqrt(spread + EPSILON) * gain_vec + bias_vec


def gelu_tanh(values):
    return jax.nn.gelu(values, approximate=True)


def norm_back(inputs, gain_vec, bias_vec, upstream):
    pullback = jax.vjp(layer_norm, inputs, gain_vec, bias_vec)[1]
    return pullback(upstream)


def columns(blocks, first, count):
    width = blocks.shape[0]
    return blocks[:, first * width : (first + count) * width]


def softmax_back(attend, upstream):
    return attend * (upstream - jnp.sum(upstream * attend, axis=-1, keepdims=True))


def feed_inner(blocks, scales, latent, column, block):
    hidden = lowered(layer_norm(latent, scales[:, column], scales[:, column + 1]))
    before = matmul(hidden, columns(blocks, block, 1))
    active = lowered(gelu_tanh(before))
    return (latent + matmul(active, columns(blocks, block + 1, 1)), (hidden, before, active))


def feed_back(blocks, scales, latent, upstream, column, block):
    hidden, before, active = feed_inner(blocks, scales, latent, column, block)[1]
    grad_low = lowered(upstream)
    grad_active = right_dot(grad_low, columns(blocks, block + 1, 1))
    pullback = jax.vjp(gelu_tanh, before)[1]
    grad_before = lowered(pullback(grad_active)[0])
    grad_input, grad_gain, grad_bias = norm_back(
        latent,
        scales[:, column],
        scales[:, column + 1],
        right_dot(grad_before, columns(blocks, block, 1)),
    )
    mat_grads = {block: left_dot(hidden, grad_before), block + 1: left_dot(active, grad_low)}
    return (upstream + grad_input, mat_grads, {column: grad_gain, column + 1: grad_bias})


def cross_inner(blocks, scales, key_value, latent):
    width = latent.shape[1]
    hidden = lowered(layer_norm(latent, scales[:, 0], scales[:, 1]))
    queries = lowered(matmul(hidden, columns(blocks, 0, 1)))
    scores = right_dot(queries, key_value[:, :width]) * width ** (-0.5)
    attend = jax.nn.softmax(scores, axis=-1)
    attend_low = lowered(attend)
    blended = lowered(matmul(attend_low, key_value[:, width:]))
    middle = latent + matmul(blended, columns(blocks, 1, 1))
    return (middle, (hidden, queries, attend, attend_low, blended))


def cross_back(blocks, scales, key_value, latent, upstream):
    width = latent.shape[1]
    middle, (hidden, queries, attend, attend_low, blended) = cross_inner(
        blocks, scales, key_value, latent
    )
    grad_middle, mat_grads, gain_grads = feed_back(blocks, scales, middle, upstream, 2, 2)
    grad_low = lowered(grad_middle)
    mat_grads[1] = left_dot(blended, grad_low)
    grad_blended = lowered(right_dot(grad_low, columns(blocks, 1, 1)))
    grad_attend = right_dot(grad_blended, key_value[:, width:])
    grad_values = left_dot(attend_low, grad_blended)
    grad_scores = lowered(softmax_back(attend, grad_attend) * width ** (-0.5))
    grad_queries = lowered(matmul(grad_scores, key_value[:, :width]))
    grad_keys = left_dot(grad_scores, queries)
    mat_grads[0] = left_dot(hidden, grad_queries)
    grad_input, gain_grads[0], gain_grads[1] = norm_back(
        latent, scales[:, 0], scales[:, 1], right_dot(grad_queries, columns(blocks, 0, 1))
    )
    return (
        grad_middle + grad_input,
        mat_grads,
        gain_grads,
        jnp.concatenate([grad_keys, grad_values], axis=1),
    )


def latent_inner(blocks, scales, latent):
    tokens, width = latent.shape
    hidden = lowered(layer_norm(latent, scales[:, 4], scales[:, 5]))
    packed = lowered(matmul(hidden, columns(blocks, 4, 3))).reshape(
        tokens, 3, HEADS, width // HEADS
    )
    scores = jnp.einsum(
        "lhe,mhe->hlm", packed[:, 0], packed[:, 1], preferred_element_type=jnp.float32
    ) * (width // HEADS) ** (-0.5)
    attend = jax.nn.softmax(scores, axis=-1)
    attend_low = lowered(attend)
    blended = lowered(
        jnp.einsum("hlm,mhe->lhe", attend_low, packed[:, 2], preferred_element_type=jnp.float32)
    ).reshape(tokens, width)
    middle = latent + matmul(blended, columns(blocks, 7, 1))
    return (middle, (hidden, packed, attend, attend_low, blended))


def latent_back(blocks, scales, latent, upstream):
    tokens, width = latent.shape
    middle, (hidden, packed, attend, attend_low, blended) = latent_inner(blocks, scales, latent)
    grad_middle, mat_grads, gain_grads = feed_back(blocks, scales, middle, upstream, 6, 8)
    grad_low = lowered(grad_middle)
    mat_grads[7] = left_dot(blended, grad_low)
    grad_blended = lowered(right_dot(grad_low, columns(blocks, 7, 1))).reshape(
        tokens, HEADS, width // HEADS
    )
    grad_attend = jnp.einsum(
        "lhe,mhe->hlm", grad_blended, packed[:, 2], preferred_element_type=jnp.float32
    )
    grad_values = jnp.einsum(
        "hlm,lhe->mhe", attend_low, grad_blended, preferred_element_type=jnp.float32
    )
    grad_scores = lowered(softmax_back(attend, grad_attend) * (width // HEADS) ** (-0.5))
    grad_queries = jnp.einsum(
        "hlm,mhe->lhe", grad_scores, packed[:, 1], preferred_element_type=jnp.float32
    )
    grad_keys = jnp.einsum(
        "hlm,lhe->mhe", grad_scores, packed[:, 0], preferred_element_type=jnp.float32
    )
    grad_packed = lowered(
        jnp.stack([grad_queries, grad_keys, grad_values], axis=1).reshape(tokens, 3 * width)
    )
    mat_grads[4] = left_dot(hidden, grad_packed)
    grad_input, gain_grads[4], gain_grads[5] = norm_back(
        latent, scales[:, 4], scales[:, 5], right_dot(grad_packed, columns(blocks, 4, 3))
    )
    return (grad_middle + grad_input, mat_grads, gain_grads)


def crop_forward(fetcher, key_value, latent):
    stored = []
    blocks, scales = fetcher(0)
    stored.append(latent)
    middle = cross_inner(blocks, scales, key_value, latent)[0]
    latent = feed_inner(blocks, scales, middle, 2, 2)[0]
    stored.append(latent)
    middle = latent_inner(blocks, scales, latent)[0]
    latent = feed_inner(blocks, scales, middle, 6, 8)[0]
    return (latent, stored, scales)


def add_into(totals, parts):
    for member in parts:
        totals[member] = totals[member] + parts[member] if member in totals else parts[member]


def reduce_owner(full):
    n_wide = lax.axis_size("wide")
    n_narrow = lax.axis_size("narrow")
    rows, cols = full.shape
    piece = rows // (n_wide * n_narrow)
    sectioned = full.reshape(1, n_wide, n_narrow, piece, cols)
    first = lax.all_to_all(
        sectioned.astype(jnp.bfloat16), "narrow", split_axis=2, concat_axis=0, tiled=True
    ).astype(sectioned.dtype)
    partial_rows = jnp.sum(first, axis=0).reshape(1, n_wide, piece, cols)
    second = lax.all_to_all(
        partial_rows.astype(jnp.bfloat16), "wide", split_axis=1, concat_axis=0, tiled=True
    ).astype(partial_rows.dtype)
    return jnp.sum(second, axis=0).reshape(piece, cols)


def on_device(
    pixels,
    labels,
    partner,
    pair_on,
    step_count,
    matrices,
    kv_weight,
    norm_gains,
    head_weight,
    latent_init,
    matrices_first,
    kv_first,
    gains_first,
    head_first,
    latent_first,
    matrices_second,
    kv_second,
    gains_second,
    head_second,
    latent_second,
):
    axis_count = lax.axis_size(("wide", "narrow"))
    micro_count = pixels.shape[0]
    examples = axis_count * pixels.shape[1]
    kv_low, head_low, initial_low = (
        lax.all_gather(lowered(kv_weight), ("wide", "narrow"), axis=0, tiled=True),
        lax.all_gather(lowered(head_weight), ("wide", "narrow"), axis=0, tiled=True),
        lax.all_gather(lowered(latent_init), ("wide", "narrow"), axis=0, tiled=True),
    )
    initial = initial_low.astype(jnp.float32).T
    shards_low = (lowered(matrices), lowered(norm_gains))

    def forward_blocks(repeat):
        blocks, scales = (
            lax.all_gather(shards_low[0], ("wide", "narrow"), axis=0, tiled=True),
            lax.all_gather(shards_low[1], ("wide", "narrow"), axis=0, tiled=True),
        )
        return (blocks, scales.astype(jnp.float32))

    states = []
    pooled_list = []
    for position in range(micro_count):
        key_value = lowered(right_dot(pixels[position, 0], kv_low))
        result, stored, scales = crop_forward(forward_blocks, key_value, initial)
        pooled_list.append(
            lowered(jnp.mean(layer_norm(result, scales[:, 8], scales[:, 9]), axis=0))
        )
        states.append((key_value, stored, result))
    pooled_own = jnp.stack(pooled_list)
    width = pooled_own.shape[1]
    gathered = lax.all_gather(pooled_own[None], ("wide", "narrow"), axis=0, tiled=True)
    counts = lax.psum(pair_on[:, 0], ("wide", "narrow"))
    logits = matmul(pooled_own, head_low)
    label_hot = (labels[:, 0][:, None] == jnp.arange(logits.shape[1])[None, :]).astype(jnp.float32)
    cross_entropy = jax.nn.logsumexp(logits, axis=-1) - jnp.sum(logits * label_hot, axis=-1)
    partner_rows = gathered[partner[:, 0], jnp.arange(micro_count)].astype(jnp.float32)
    distance = pooled_own.astype(jnp.float32) - partner_rows
    active = pair_on[:, 0].astype(jnp.float32)
    divisor = jnp.maximum(counts, 1).astype(jnp.float32) * width**0.5
    agreement = active * jnp.sum(distance * distance, axis=-1) / divisor
    loss_local = jnp.sum(cross_entropy / examples + agreement) / micro_count
    grad_logits = lowered((jax.nn.softmax(logits, axis=-1) - label_hot) / (examples * micro_count))
    pull_term = 2.0 / micro_count * (active / divisor)[:, None] * distance
    partner_hot = (partner[:, 0][:, None] == jnp.arange(axis_count)[None, :]).astype(jnp.float32)
    returned = jnp.einsum("mn,md->nmd", partner_hot, -pull_term)
    grad_pooled = (
        right_dot(grad_logits, head_low)
        + pull_term
        + lax.psum_scatter(returned, ("wide", "narrow"), scatter_dimension=0, tiled=True)[0]
    )
    grad_head = left_dot(pooled_own, grad_logits)

    def backward_blocks():
        blocks, scales = (
            lax.all_gather(shards_low[0], ("wide", "narrow"), axis=0, tiled=True),
            lax.all_gather(shards_low[1], ("wide", "narrow"), axis=0, tiled=True),
        )
        return (blocks, scales.astype(jnp.float32))

    mat_total = {}
    gain_total = {}
    grad_kv = jnp.zeros(kv_low.shape, jnp.float32)
    grad_initial = jnp.zeros(initial.shape, jnp.float32)
    for position in range(micro_count):
        key_value, stored, result = states[position]
        blocks, scales = backward_blocks()
        spread_grad = jnp.broadcast_to(grad_pooled[position] / result.shape[0], result.shape)
        upstream, grad_gain, grad_bias = norm_back(result, scales[:, 8], scales[:, 9], spread_grad)
        add_into(gain_total, {8: grad_gain, 9: grad_bias})
        grad_pairs = jnp.zeros((key_value.shape[0], 2 * width), jnp.float32)
        for repeat in reversed(range(REPEATS)):
            upstream, mat_grads, gain_grads = latent_back(
                blocks, scales, stored[2 * repeat + 1], upstream
            )
            add_into(mat_total, mat_grads)
            add_into(gain_total, gain_grads)
            upstream, mat_grads, gain_grads, pair_part = cross_back(
                blocks, scales, key_value, stored[2 * repeat], upstream
            )
            add_into(mat_total, mat_grads)
            add_into(gain_total, gain_grads)
            grad_pairs = pair_part
        grad_kv = grad_kv + left_dot(lowered(grad_pairs), pixels[position, 0])
        grad_initial = grad_initial + upstream
    grad_matrices = jnp.concatenate(
        [
            mat_total[0],
            mat_total[1],
            mat_total[2],
            mat_total[3],
            mat_total[4],
            mat_total[7],
            mat_total[8],
            mat_total[9],
        ],
        axis=1,
    )
    grad_gains = jnp.stack([gain_total[column] for column in range(10)], axis=1)
    channels = grad_kv.shape[1]
    kv_paired = grad_kv.reshape(width, 2 * channels)
    widths_all = [
        grad_matrices.shape[1],
        2 * channels,
        grad_gains.shape[1],
        grad_head.shape[1],
        grad_initial.shape[0],
    ]
    joined = jnp.concatenate(
        [grad_matrices, kv_paired, grad_gains, grad_head, grad_initial.T], axis=1
    )
    owned = reduce_owner(joined)
    pieces = []
    offset = 0
    for span in widths_all:
        pieces.append(owned[:, offset : offset + span])
        offset = offset + span
    pieces[1] = pieces[1].reshape(2 * owned.shape[0], channels)
    shares = tuple(pieces)
    square = jnp.zeros((), jnp.float32)
    for member in shares:
        square = square + jnp.sum(member * member)
    square, total_loss = lax.psum((square, loss_local), ("wide", "narrow"))
    grad_norm = jnp.sqrt(square)
    factor = jnp.minimum(1.0, THRESH / grad_norm)
    correction = 1.0 - jnp.power(0.5, step_count[0].astype(jnp.float32))
    masters = (matrices, kv_weight, norm_gains, head_weight, latent_init)
    firsts = (matrices_first, kv_first, gains_first, head_first, latent_first)
    seconds = (matrices_second, kv_second, gains_second, head_second, latent_second)
    results = []
    for index, (grad_item, master, moment_one, moment_two) in enumerate(
        zip(shares, masters, firsts, seconds)
    ):
        clipped = grad_item * factor
        moment_one = 0.5 * moment_one + 0.5 * clipped
        moment_two = 0.5 * moment_two + 0.5 * clipped * clipped
        if index == 2 or index == 4:
            results = results + [moment_one, moment_two, clipped]
        else:
            master = master - RATE * (
                moment_one / correction / (jnp.sqrt(moment_two / correction) + TINY)
                + DECAY * master
            )
            results = results + [moment_one, moment_two, master]
    return (
        total_loss,
        grad_norm,
        counts,
        results[0],
        results[1],
        results[2],
        results[3],
        results[4],
        results[5],
        results[6],
        results[7],
        results[8],
        results[9],
        results[10],
        results[11],
        results[12],
        results[13],
        results[14],
    )


def solution(mesh):
    in_specs = (
        P(None, ("wide", "narrow"), None, None),
        P(None, ("wide", "narrow")),
        P(None, ("wide", "narrow")),
        P(None, ("wide", "narrow")),
        P(),
        P(("wide", "narrow"), None),
        P(("wide", "narrow"), None),
        P(("wide", "narrow"), None),
        P(("wide", "narrow"), None),
        P(("wide", "narrow"), None),
        P(("wide", "narrow"), None),
        P(("wide", "narrow"), None),
        P(("wide", "narrow"), None),
        P(("wide", "narrow"), None),
        P(("wide", "narrow"), None),
        P(("wide", "narrow"), None),
        P(("wide", "narrow"), None),
        P(("wide", "narrow"), None),
        P(("wide", "narrow"), None),
        P(("wide", "narrow"), None),
    )
    out_specs = (
        P(),
        P(),
        P(),
        P(("wide", "narrow"), None),
        P(("wide", "narrow"), None),
        P(("wide", "narrow"), None),
        P(("wide", "narrow"), None),
        P(("wide", "narrow"), None),
        P(("wide", "narrow"), None),
        P(("wide", "narrow"), None),
        P(("wide", "narrow"), None),
        P(("wide", "narrow"), None),
        P(("wide", "narrow"), None),
        P(("wide", "narrow"), None),
        P(("wide", "narrow"), None),
        P(("wide", "narrow"), None),
        P(("wide", "narrow"), None),
        P(("wide", "narrow"), None),
    )
    return jax.shard_map(
        on_device, mesh=mesh, in_specs=in_specs, out_specs=out_specs, check_vma=False
    )
```

profile of v0, /device:TPU:0, one launch (start us, length us, event | category | flops | bytes accessed | tf_op | source)
XLA Modules:
  0.0 1591.0 jit_solution(13490384611529241700)
XLA Ops:
  13.6 42.1 %psum.21 = s32[2]{0:T(128)S(1)} all-reduce(s32[2]{0:T(128)S(1)} %bitcast.344), channel_id=1, replica_groups=mesh['wide'=16,'narrow'=2] {'wide','narrow'}, use_global_device_ids=true, to_apply=%region_32.0 | all-reduce | flops 2 | bytes 16 | tf_op jit(solution)/shard_map/psum | solution.py:257
  56.2 66.7 %all-gather.1 = bf16[32,32,10]{1,2,0:T(8,128)(2,1)S(1)} all-gather(bf16[1,32,10]{1,2,0:T(8,128)(2,1)S(1)} %convert_bitcast_fusion.1), channel_id=1, replica_groups=mesh['wide'=16,'narrow'=2] {'wide','narrow'}, dimensions={0}, use_global_device_ids=true | all-gather | bytes 21120 | tf_op jit(solution)/shard_map/all_gather | solution.py:241
  131.0 131.5 %all-gather.10.cloned.1.call-done = bf16[1024,10240]{1,0:T(8,128)(2,1)} async-done(((bf16[32,10240]{1,0:T(8,128)(2,1)}), bf16[1024,10240]{1,0:T(8,128)(2,1)}) %all-gather.10.cloned.1.call-update) | async-done | bytes 20971536 | tf_op jit(solution)/shard_map/all_gather | solution.py:240
  302.7 7.1 fusion.123
  323.5 9.2 fusion.132
  353.1 10.3 fusion.138
  383.8 66.2 %all-gather.2 = bf16[32,2,1024]{2,1,0:T(2,128)(2,1)S(1)} all-gather(bf16[1,2,1024]{2,1,0:T(2,128)(2,1)S(1)} %fusion.417), channel_id=2, replica_groups=mesh['wide'=16,'narrow'=2] {'wide','narrow'}, dimensions={0}, use_global_device_ids=true | all-gather | bytes 135168 | tf_op jit(solution)/shard_map/all_gather | solution.py:256
  462.2 111.0 %all-reduce.4.cloned.1.call-done = f32[32,2,1024]{2,1,0:T(2,128)} async-done(((f32[32,2,1024]{2,1,0:T(2,128)}), f32[32,2,1024]{2,1,0:T(2,128)}) %all-reduce.4.cloned.1.call-update) | async-done | bytes 262160
  612.7 9.0 fusion.171
  626.4 15.4 fusion.168
  641.8 16.1 %fusion.165 = bf16[512,1,8,128]{0,3,2,1:T(8,128)(2,1)} fusion(f32[8,512,512]{1,2,0:T(8,128)} %fusion.238, bf16[512,1,8,128]{3,2,1,0:T(8,128)(2,1)} %get-tuple-element.173, f32[8,512,512]{1,2,0:T(8,128)} %get-tuple-element.226, f32[8,512]{1,0:T(8,128)S(1)} %get-tuple-element.225), kind=kOutput, calls=%fused_computation.244 | convolution fusion | flops 552079872 | bytes 18890752 | tf_op jit(solution)/shard_map/hlm,lhe->mhe/dot_general | solution.py:159
  666.9 8.8 fusion.174
  680.4 15.3 fusion.162
  695.7 13.6 fusion.159
  718.4 8.3 multiply_reduce_fusion.8
  775.1 7.9 fusion.313
  841.3 7.7 fusion.89
  864.4 8.9 add_convert_fusion
  879.6 43.3 %concatenate.89 = bf16[1,16,2,32,12284]{4,3,1,0,2:T(8,128)(2,1)} concatenate(bf16[1,16,2,32,1024]{4,3,1,0,2:T(8,128)(2,1)} %copy.205, bf16[1,16,2,32,1024]{4,3,1,0,2:T(8,128)(2,1)} %copy.206, bf16[1,16,2,32,1024]{4,3,1,0,2:T(8,128)(2,1)} %copy.207, bf16[1,16,2,32,1024]{4,3,1,0,2:T(8,128)(2,1)} %copy.208, bf16[1,16,2,32,3072]{4,3,1,0,2:T(8,128)(2,1)} %copy.209, ...), dimensions={4} | concatenate | bytes 50315264 | tf_op jit(solution)/shard_map/concatenate | solution.py:333
  922.9 296.8 %all_to_all.8 = bf16[1,16,2,32,12284]{4,3,1,0,2:T(8,128)(2,1)} all-to-all(bf16[1,16,2,32,12284]{4,3,1,0,2:T(8,128)(2,1)} %concatenate.89), channel_id=1, replica_groups=mesh['wide'=16,'narrow'=2] {'narrow'}, dimensions={2} | all-to-all | bytes 50315264 | tf_op jit(solution)/shard_map/all_to_all | solution.py:195
  1219.7 21.2 %reduce_sum.812 = bf16[16,32,12284]{2,1,0:T(8,128)(2,1)} reduce(bf16[1,16,2,32,12284]{4,3,1,0,2:T(8,128)(2,1)} %all_to_all.8, bf16[]{:T(256)} %constant.118.clone.1), dimensions={0,2}, to_apply=%region_79.0 | reduce | flops 6289408 | bytes 37736448 | tf_op jit(solution)/shard_map/reduce_sum | solution.py:198
  1248.4 221.5 %all-to-all-done.1 = bf16[1,16,32,12284]{3,2,0,1:T(8,128)(2,1)} async-done(((bf16[1,16,32,12284]{3,2,0,1:T(8,128)(2,1)}), bf16[1,16,32,12284]{3,2,0,1:T(8,128)(2,1)}, u32[]{:S(2)}, u32[]{:S(2)}) %all-to-all-start.1) | async-done | bytes 12578848 | tf_op jit(solution)/shard_map/all_to_all | solution.py:199
  1469.8 7.0 convert_reduce_fusion
  1483.8 88.4 %all-reduce.1 = (f32[]{:T(128)}, f32[]{:T(128)}) all-reduce(f32[]{:T(128)S(6)} %div.365, f32[]{:T(128)S(6)} %add.762), channel_id=1, replica_groups=mesh['wide'=16,'narrow'=2] {'wide','narrow'}, use_global_device_ids=true, to_apply=%region_34.0 | all-reduce | flops 2 | bytes 16 | tf_op jit(solution)/shard_map/psum | solution.py:347
  (703 shorter events, 333.8 us)
Async XLA Ops:
  7.2 117.1 %all-gather.8.cloned.1.call-start = ((), (), s32[]{:S(2)}) async-start(), calls=%async_computation.2 | async-start | bytes 1081344 | tf_op jit(solution)/shard_map/all_gather | solution.py:233
  8.9 117.9 %all-gather.12.cloned.1.call-start = ((), (), s32[]{:S(2)}) async-start(), calls=%async_computation.4 | async-start | bytes 1622016 | tf_op jit(solution)/shard_map/all_gather | solution.py:231
  10.5 252.1 %all-gather.10.cloned.1.call-start = ((), (), s32[]{:S(2)}) async-start(), calls=%async_computation.3 | async-start | bytes 21626880 | tf_op jit(solution)/shard_map/all_gather | solution.py:240
  12.8 368.9 %all-gather.14.cloned.1.call-start = ((), (), s32[]{:S(2)}) async-start(), calls=%async_computation.5 | async-start | bytes 2162688 | tf_op jit(solution)/shard_map/all_gather | solution.py:232
  13.5 559.6 %all-reduce.4.cloned.1.call-start = ((), (), s32[]{:S(2)}) async-start(), calls=%async_computation.6 | async-start | bytes 524288
  123.6 138.9 %copy-start.123 = (f32[1024,1]{0,1:T(1,128)}, f32[1024,1]{0,1:T(1,128)S(1)}, u32[]{:S(2)}) copy-start(f32[1024,1]{0,1:T(1,128)S(1)} %get-tuple-element.190) | copy-start | bytes 12292
  123.6 138.9 %copy-start.199 = (f32[1024,1]{0,1:T(1,128)}, f32[1024,1]{0,1:T(1,128)S(1)}, u32[]{:S(2)}) copy-start(f32[1024,1]{0,1:T(1,128)S(1)} %get-tuple-element.189) | copy-start | bytes 12292
  123.7 169.7 %copy-start.127 = (f32[1024,1]{0,1:T(1,128)}, f32[1024,1]{0,1:T(1,128)S(1)}, u32[]{:S(2)}) copy-start(f32[1024,1]{0,1:T(1,128)S(1)} %get-tuple-element.188) | copy-start | bytes 12292
  123.7 169.7 %copy-start.201 = (f32[1024,1]{0,1:T(1,128)}, f32[1024,1]{0,1:T(1,128)S(1)}, u32[]{:S(2)}) copy-start(f32[1024,1]{0,1:T(1,128)S(1)} %get-tuple-element.187) | copy-start | bytes 12292
  123.7 179.0 %copy-start.121 = (f32[1024,1]{0,1:T(1,128)}, f32[1024,1]{0,1:T(1,128)S(1)}, u32[]{:S(2)}) copy-start(f32[1024,1]{0,1:T(1,128)S(1)} %get-tuple-element.186) | copy-start | bytes 12292
  123.7 480.9 %copy-start.125 = (f32[1024,1]{0,1:T(1,128)}, f32[1024,1]{0,1:T(1,128)S(1)}, u32[]{:S(2)}) copy-start(f32[1024,1]{0,1:T(1,128)S(1)} %get-tuple-element.184) | copy-start | bytes 12292
  126.1 147.5 %copy-start.6 = (bf16[1024,512]{0,1:T(8,128)(2,1)}, bf16[1024,512]{0,1:T(8,128)(2,1)S(1)}, u32[]{:S(2)}) copy-start(bf16[1024,512]{0,1:T(8,128)(2,1)S(1)} %copy.174) | copy-start | bytes 3145732
  129.1 139.9 %copy-start.89 = (bf16[272,2048]{1,0:T(8,128)(2,1)}, bf16[272,2048]{1,0:T(8,128)(2,1)S(1)}, u32[]{:S(2)}) copy-start(bf16[272,2048]{1,0:T(8,128)(2,1)S(1)} %convolution_convert_fusion.2) | copy-start | bytes 3342340
  337.0 267.6 %copy-start.143 = (f32[512]{0:T(512)}, f32[512]{0:T(512)S(1)}, u32[]{:S(2)}) copy-start(f32[512]{0:T(512)S(1)} %broadcast_multiply_fusion.5) | copy-start | bytes 6148
  337.3 267.3 %copy-start.169 = (f32[512]{0:T(512)}, f32[512]{0:T(512)S(1)}, u32[]{:S(2)}) copy-start(f32[512]{0:T(512)S(1)} %fusion.285) | copy-start | bytes 6148
  345.9 312.1 %copy-start.110 = (f32[512]{0:T(512)}, f32[512]{0:T(512)S(1)}, u32[]{:S(2)}) copy-start(f32[512]{0:T(512)S(1)} %broadcast_multiply_fusion.4) | copy-start | bytes 6148
  369.5 235.1 %copy-start.145 = (f32[512]{0:T(512)}, f32[512]{0:T(512)S(1)}, u32[]{:S(2)}) copy-start(f32[512]{0:T(512)S(1)} %broadcast_multiply_fusion.1) | copy-start | bytes 6148
  369.9 234.7 %copy-start.171 = (f32[512]{0:T(512)}, f32[512]{0:T(512)S(1)}, u32[]{:S(2)}) copy-start(f32[512]{0:T(512)S(1)} %fusion.289) | copy-start | bytes 6148
  378.4 228.7 %copy-start = (f32[512,1024]{1,0:T(8,128)}, f32[512,1024]{1,0:T(8,128)S(1)}, u32[]{:S(2)}) copy-start(f32[512,1024]{1,0:T(8,128)S(1)} %get-tuple-element.156) | copy-start | bytes 6291460
  378.4 228.7 %copy-start.112 = (f32[512]{0:T(512)}, f32[512]{0:T(512)S(1)}, u32[]{:S(2)}) copy-start(f32[512]{0:T(512)S(1)} %broadcast_multiply_fusion) | copy-start | bytes 6148
  378.8 279.1 %copy-start.117 = (f32[512]{0:T(512)}, f32[512]{0:T(512)S(1)}, u32[]{:S(2)}) copy-start(f32[512]{0:T(512)S(1)} %fusion.286) | copy-start | bytes 6148
  378.8 228.3 %copy-start.119 = (f32[512]{0:T(512)}, f32[512]{0:T(512)S(1)}, u32[]{:S(2)}) copy-start(f32[512]{0:T(512)S(1)} %fusion.290) | copy-start | bytes 6148
  383.8 189.3 %copy-start.197 = (f32[2]{0:T(128)}, f32[2]{0:T(128)S(1)}, u32[]{:S(2)}) copy-start(f32[2]{0:T(128)S(1)} %get-tuple-element.229) | copy-start | bytes 28
  1241.0 228.8 %all-to-all-start.1 = ((bf16[1,16,32,12284]{3,2,0,1:T(8,128)(2,1)}), bf16[1,16,32,12284]{3,2,0,1:T(8,128)(2,1)}, u32[]{:S(2)}, u32[]{:S(2)}) async-start(bf16[1,16,32,12284]{3,2,0,1:T(8,128)(2,1)} %bitcast.274), calls=%async_computation.1 | async-start | bytes 25165824 | tf_op jit(solution)/shard_map/all_to_all | solution.py:199
  (210 other events, 2416.1 us)
Sparse Core Ops, SparseCore 0:
  11.5 56.4 all-gather.7
  71.5 54.0 all-gather.11
  129.0 133.4 all-gather.9
  266.0 54.6 all-gather.13
  452.2 120.8 all-reduce.3
where the time goes:
time: 1600 us; the launch traced here: 1590 us
  blocking collectives  560 us (35%)
  waiting for transfers between devices  464 us (29%)
  matrix products  327 us (20%)
  local copies, waits for them, and re-layouts  120 us (8%)
  other arithmetic  90.6 us (6%)
  between operations  23.8 us (1%)
    all_to_all x1, blocking collectives, reduce_owner(): lax.all_to_all(sectioned.astype(jnp.bfloat16), 'narrow', split_axis=2, co...  297 us
    all_to_all x1, waiting for transfers between devices, reduce_owner(): lax.all_to_all(partial_rows.astype(jnp.bfloat16), 'wide', split_axis=1, c...  221 us
    all_gather x1, waiting for transfers between devices, forward_blocks(): lax.all_gather(shards_low[0], ('wide', 'narrow'), axis=0, tiled=True)  132 us
    unnamed x6, waiting for transfers between devices  111 us
    psum x1, blocking collectives, on_device(): square, total_loss = lax.psum((square, loss_local), ('wide', 'narrow'))  88.4 us
    concatenate x33, local copies, waits for them, and re-layouts, on_device(): jnp.concatenate([grad_matrices, kv_paired, grad_gains, grad_head, grad_in...  80.5 us
    dot_general x23, matrix products, right_dot(): lax.dot_general(first_op, second_op, (((1,), (1,)), ((), ())), preferred_...  77.9 us
    dot_general x23, matrix products, left_dot(): lax.dot_general(first_op, second_op, (((0,), (0,)), ((), ())), preferred_...  73.5 us
  transfers between devices with their start and end apart: 6, of which 3 were waited for; matrix products, arithmetic and copies ran while one was open for 8% of the time, Pallas kernels for 0%

commit v1 on v0

v1 whole, which is shorter than its diff:
```python
import jax
import jax.numpy as jnp
from jax import lax
from jax.sharding import PartitionSpec as P

HEADS = 8
AXES = ("wide", "narrow")


EPSILON = 1e-05
RATE = 0.03
DECAY = 0.1
TINY = 1e-08
THRESH = 0.01


def lowered(values):
    return values.astype(jnp.bfloat16)


def matmul(first_op, second_op):
    return jnp.dot(first_op, second_op, preferred_element_type=jnp.float32)


def left_dot(first_op, second_op):
    return lax.dot_general(
        first_op, second_op, (((0,), (0,)), ((), ())), preferred_element_type=jnp.float32
    )


def right_dot(first_op, second_op):
    return lax.dot_general(
        first_op, second_op, (((1,), (1,)), ((), ())), preferred_element_type=jnp.float32
    )


def layer_norm(inputs, gain_vec, bias_vec):
    center = inputs - jnp.mean(inputs, axis=-1, keepdims=True)
    spread = jnp.mean(center * center, axis=-1, keepdims=True)
    return center * lax.rsqrt(spread + EPSILON) * gain_vec + bias_vec


def gelu_tanh(values):
    return jax.nn.gelu(values, approximate=True)


def norm_back(inputs, gain_vec, bias_vec, upstream):
    pullback = jax.vjp(layer_norm, inputs, gain_vec, bias_vec)[1]
    return pullback(upstream)


def softmax_back(attend, upstream):
    return attend * (upstream - jnp.sum(upstream * attend, axis=-1, keepdims=True))


def digits():
    n_wide = lax.axis_size("wide")
    n_narrow = lax.axis_size("narrow")
    rest = n_wide // 2
    top = min(4, rest)
    return (
        ("z", n_narrow * n_wide // top, top),
        ("y", 2 * n_narrow, rest // top),
        ("c", n_narrow, 2),
        ("x", 1, n_narrow),
    )


def device_index():
    return lax.axis_index("wide") * lax.axis_size("narrow") + lax.axis_index("narrow")


def exchange(values, offset):
    total = lax.axis_size(AXES)
    return lax.ppermute(values, AXES, [(i, i ^ offset) for i in range(total)])


def in_place(pieces, mine, axis):
    stacked = jnp.stack(pieces, axis=axis)
    bit = 1
    while bit < len(pieces):
        swapped = jnp.stack(
            [lax.index_in_dim(stacked, k ^ bit, axis, keepdims=False) for k in range(len(pieces))],
            axis=axis,
        )
        stacked = jnp.where((mine & bit) != 0, swapped, stacked)
        bit = bit * 2
    return stacked


def gather_rows(shard, order):
    me = device_index()
    table = digits()
    present = []
    current = shard
    for name in order:
        place = [entry[0] for entry in table].index(name)
        _, stride, size = table[place]
        if size == 1:
            continue
        mine = (me // stride) % size
        pieces = [current] + [exchange(current, k * stride) for k in range(1, size)]
        axis = sum(1 for other in present if other < place)
        present.append(place)
        current = in_place(pieces, mine, axis)
    return current.reshape((-1,) + shard.shape[1:])


def scatter_rows(full, order):
    me = device_index()
    table = digits()
    total = lax.axis_size(AXES)
    rows = full.shape[0] // total
    current = full.reshape(tuple(entry[2] for entry in table) + (rows,) + full.shape[1:])
    left = [entry[0] for entry in table]
    for name in order:
        place = [entry[0] for entry in table].index(name)
        _, stride, size = table[place]
        axis = left.index(name)
        left.remove(name)
        mine = (me // stride) % size
        kept = lax.dynamic_index_in_dim(current, mine, axis, keepdims=False).astype(jnp.float32)
        for k in range(1, size):
            sent = lax.dynamic_index_in_dim(current, mine ^ k, axis, keepdims=False)
            kept = kept + exchange(sent, k * stride).astype(jnp.float32)
        current = kept if not left else lowered(kept)
    return current


def gather_small(values):
    total = lax.axis_size(AXES)
    me = device_index()
    current = values[None]
    done = 1
    while done < total:
        step = min(8, total // done)
        current = jnp.concatenate(
            [current] + [exchange(current, k * done) for k in range(1, step)], axis=0
        )
        done = done * step
    return jnp.take(current, jnp.arange(total) ^ me, axis=0)


def feed_inner(first, second, gain_vec, bias_vec, latent):
    hidden = lowered(layer_norm(latent, gain_vec, bias_vec))
    before = matmul(hidden, first)
    active = lowered(gelu_tanh(before))
    return (latent + matmul(active, second), (hidden, before, active))


def feed_back(first, second, gain_vec, bias_vec, latent, stored, upstream):
    hidden, before, active = stored
    grad_low = lowered(upstream)
    grad_second = lowered(left_dot(active, grad_low))
    grad_active = right_dot(grad_low, second)
    pullback = jax.vjp(gelu_tanh, before)[1]
    grad_before = lowered(pullback(grad_active)[0])
    grad_first = lowered(left_dot(hidden, grad_before))
    grad_input, grad_gain, grad_bias = norm_back(
        latent, gain_vec, bias_vec, right_dot(grad_before, first)
    )
    return (upstream + grad_input, grad_first, grad_second, grad_gain, grad_bias)


def on_device(
    pixels,
    labels,
    partner,
    pair_on,
    step_count,
    matrices,
    kv_weight,
    norm_gains,
    head_weight,
    latent_init,
    matrices_first,
    kv_first,
    gains_first,
    head_first,
    latent_first,
    matrices_second,
    kv_second,
    gains_second,
    head_second,
    latent_second,
):
    axis_count = lax.axis_size(AXES)
    me = device_index()
    micro_count, _, spots, _ = pixels.shape
    examples = axis_count
    tokens = latent_init.shape[1]
    width = matrices.shape[1] // 10
    own_rows = matrices.shape[0]
    part = width // HEADS
    first_order = ("z", "y", "x", "c")
    second_order = ("z", "x", "y", "c")

    small = jnp.pad(
        jnp.concatenate([lowered(latent_init), lowered(norm_gains)], axis=1),
        ((0, 0), (0, 128 - norm_gains.shape[1])),
    )
    small = gather_rows(small, first_order)
    kv_low = gather_rows(lowered(kv_weight), second_order)
    weights = {}
    for turn, (block, count) in enumerate(
        ((0, 1), (1, 1), (2, 1), (3, 1), (4, 3), (7, 1), (8, 1), (9, 1))
    ):
        weights[block] = gather_rows(
            lowered(matrices[:, block * width : (block + count) * width]),
            first_order if turn % 2 == 0 else second_order,
        )
    head_low = gather_rows(lowered(head_weight), first_order)
    marks = gather_small(jnp.concatenate([labels, partner, pair_on], axis=0)[:, 0])
    labels_all = marks[:, 0:micro_count]
    partner_all = marks[:, micro_count : 2 * micro_count]
    pair_all = marks[:, 2 * micro_count : 3 * micro_count]
    counts = jnp.sum(pair_all, axis=0)

    initial = small[:, :tokens].astype(jnp.float32).T
    scales = small[:, tokens : tokens + 10].astype(jnp.float32).T

    flat = (micro_count * tokens, width)
    split = (micro_count, tokens, width)
    pictures = pixels[:, 0]
    key_value = lowered(
        matmul(pictures.reshape(micro_count * spots, -1), kv_low.T)
    ).reshape(micro_count, spots, 2 * width)
    keys, values = key_value[:, :, :width], key_value[:, :, width:]
    hidden_zero = lowered(layer_norm(initial, scales[0], scales[1]))
    queries = lowered(matmul(hidden_zero, weights[0]))
    scores = jnp.einsum(
        "ld,mpd->mlp", queries, keys, preferred_element_type=jnp.float32
    ) * width ** (-0.5)
    attend = jax.nn.softmax(scores, axis=-1)
    attend_low = lowered(attend)
    blended = lowered(
        jnp.einsum("mlp,mpd->mld", attend_low, values, preferred_element_type=jnp.float32)
    ).reshape(flat)
    latent_one = (initial[None] + matmul(blended, weights[1]).reshape(split)).reshape(flat)
    latent_two, stored_cross = feed_inner(weights[2], weights[3], scales[2], scales[3], latent_one)
    hidden_two = lowered(layer_norm(latent_two, scales[4], scales[5]))
    packed = lowered(matmul(hidden_two, weights[4])).reshape(micro_count, tokens, 3, HEADS, part)
    scores_self = jnp.einsum(
        "blhe,bmhe->bhlm", packed[:, :, 0], packed[:, :, 1], preferred_element_type=jnp.float32
    ) * part ** (-0.5)
    attend_self = jax.nn.softmax(scores_self, axis=-1)
    attend_self_low = lowered(attend_self)
    blended_self = lowered(
        jnp.einsum(
            "bhlm,bmhe->blhe", attend_self_low, packed[:, :, 2], preferred_element_type=jnp.float32
        )
    ).reshape(flat)
    latent_three = latent_two + matmul(blended_self, weights[7])
    result, stored_self = feed_inner(weights[8], weights[9], scales[6], scales[7], latent_three)
    normed = layer_norm(result, scales[8], scales[9])
    pooled_own = lowered(jnp.mean(normed.reshape(split), axis=1))

    pooled_all = gather_small(pooled_own)
    logits = matmul(pooled_all.reshape(-1, width), head_low).reshape(axis_count, micro_count, -1)
    label_hot = (labels_all[:, :, None] == jnp.arange(logits.shape[-1])).astype(jnp.float32)
    cross_entropy = jax.nn.logsumexp(logits, axis=-1) - jnp.sum(logits * label_hot, axis=-1)
    micro_index = jnp.arange(micro_count)[None]
    pooled_wide = pooled_all.astype(jnp.float32)
    distance = pooled_wide - pooled_wide[partner_all, micro_index]
    active = pair_all.astype(jnp.float32)
    divisor = jnp.maximum(counts, 1).astype(jnp.float32) * width**0.5
    agreement = active * jnp.sum(distance * distance, axis=-1) / divisor
    total_loss = jnp.sum(cross_entropy / examples + agreement) / micro_count
    grad_logits = lowered((jax.nn.softmax(logits, axis=-1) - label_hot) / (examples * micro_count))
    pull_term = (2.0 / micro_count * (active / divisor))[:, :, None] * distance
    aimed = (partner_all == me).astype(jnp.float32)
    grad_logits_own = lax.dynamic_index_in_dim(grad_logits, me, 0, keepdims=False)
    pull_own = lax.dynamic_index_in_dim(pull_term, me, 0, keepdims=False)
    grad_pooled = (
        right_dot(grad_logits_own, head_low) + pull_own - jnp.sum(aimed[:, :, None] * pull_term, axis=0)
    )
    pooled_rows = lax.dynamic_slice_in_dim(
        pooled_all.reshape(-1, width), me * own_rows, own_rows, axis=1
    )
    grad_head = left_dot(pooled_rows, grad_logits.reshape(pooled_rows.shape[0], -1))

    orders = (("c", "x", "y", "z"), ("c", "y", "x", "z"))
    owned = {}
    gain_grads = {}
    spread_grad = jnp.broadcast_to((grad_pooled / tokens)[:, None], split).reshape(flat)
    upstream, gain_grads[8], gain_grads[9] = norm_back(result, scales[8], scales[9], spread_grad)
    upstream, first, second, gain_grads[6], gain_grads[7] = feed_back(
        weights[8], weights[9], scales[6], scales[7], latent_three, stored_self, upstream
    )
    owned[9] = scatter_rows(second, orders[0])
    owned[8] = scatter_rows(first, orders[1])
    grad_low = lowered(upstream)
    owned[7] = scatter_rows(lowered(left_dot(blended_self, grad_low)), orders[0])
    grad_blended = lowered(right_dot(grad_low, weights[7])).reshape(micro_count, tokens, HEADS, part)
    grad_attend = jnp.einsum(
        "blhe,bmhe->bhlm", grad_blended, packed[:, :, 2], preferred_element_type=jnp.float32
    )
    grad_values = jnp.einsum(
        "bhlm,blhe->bmhe", attend_self_low, grad_blended, preferred_element_type=jnp.float32
    )
    grad_scores = lowered(softmax_back(attend_self, grad_attend) * part ** (-0.5))
    grad_queries = jnp.einsum(
        "bhlm,bmhe->blhe", grad_scores, packed[:, :, 1], preferred_element_type=jnp.float32
    )
    grad_keys = jnp.einsum(
        "bhlm,blhe->bmhe", grad_scores, packed[:, :, 0], preferred_element_type=jnp.float32
    )
    grad_packed = lowered(
        jnp.stack([grad_queries, grad_keys, grad_values], axis=2).reshape(flat[0], 3 * width)
    )
    owned[4] = scatter_rows(lowered(left_dot(hidden_two, grad_packed)), orders[1])
    grad_input, gain_grads[4], gain_grads[5] = norm_back(
        latent_two, scales[4], scales[5], right_dot(grad_packed, weights[4])
    )
    upstream = upstream + grad_input
    upstream, first, second, gain_grads[2], gain_grads[3] = feed_back(
        weights[2], weights[3], scales[2], scales[3], latent_one, stored_cross, upstream
    )
    owned[3] = scatter_rows(second, orders[0])
    owned[2] = scatter_rows(first, orders[1])
    grad_low = lowered(upstream)
    owned[1] = scatter_rows(lowered(left_dot(blended, grad_low)), orders[0])
    grad_blended = lowered(right_dot(grad_low, weights[1])).reshape(split)
    grad_attend = jnp.einsum("mld,mpd->mlp", grad_blended, values, preferred_element_type=jnp.float32)
    grad_values = jnp.einsum(
        "mlp,mld->mpd", attend_low, grad_blended, preferred_element_type=jnp.float32
    )
    grad_scores = lowered(softmax_back(attend, grad_attend) * width ** (-0.5))
    grad_queries = lowered(
        jnp.einsum("mlp,mpd->mld", grad_scores, keys, preferred_element_type=jnp.float32)
    )
    grad_keys = jnp.einsum("mlp,ld->mpd", grad_scores, queries, preferred_element_type=jnp.float32)
    grad_pairs = lowered(jnp.concatenate([grad_keys, grad_values], axis=2))
    grad_kv = left_dot(
        grad_pairs.reshape(micro_count * spots, 2 * width),
        pictures.reshape(micro_count * spots, -1),
    )
    owned_kv = scatter_rows(lowered(grad_kv), orders[1])
    grad_first = jnp.einsum(
        "ld,mle->de", hidden_zero, grad_queries, preferred_element_type=jnp.float32
    )
    owned[0] = scatter_rows(lowered(grad_first), orders[0])
    grad_hidden = right_dot(grad_queries.reshape(flat), weights[0]).reshape(split)
    grad_input, gain_grads[0], gain_grads[1] = norm_back(
        initial, scales[0], scales[1], jnp.sum(grad_hidden, axis=0)
    )
    grad_initial = jnp.sum(upstream.reshape(split), axis=0) + grad_input
    gains = jnp.stack([gain_grads[column] for column in range(10)], axis=0)
    gains = jnp.pad(gains, ((0, 118), (0, 0)))
    owned_small = scatter_rows(
        lowered(jnp.concatenate([grad_initial, gains], axis=0)).T, orders[1]
    )
    grad_matrices = jnp.concatenate([owned[block] for block in (0, 1, 2, 3, 4, 7, 8, 9)], axis=1)
    shares = (
        grad_matrices,
        owned_kv,
        owned_small[:, tokens : tokens + 10],
        grad_head,
        owned_small[:, :tokens],
    )
    square = jnp.zeros((), jnp.float32)
    for member in shares:
        square = square + jnp.sum(member * member)
    square = jnp.sum(gather_small(jnp.broadcast_to(square, (128,))), axis=0)[0]
    grad_norm = jnp.sqrt(square)
    factor = jnp.minimum(1.0, THRESH / grad_norm)
    correction = 1.0 - jnp.power(0.5, step_count[0].astype(jnp.float32))
    masters = (matrices, kv_weight, norm_gains, head_weight, latent_init)
    firsts = (matrices_first, kv_first, gains_first, head_first, latent_first)
    seconds = (matrices_second, kv_second, gains_second, head_second, latent_second)
    results = []
    for index, (grad_item, master, moment_one, moment_two) in enumerate(
        zip(shares, masters, firsts, seconds)
    ):
        clipped = grad_item * factor
        moment_one = 0.5 * moment_one + 0.5 * clipped
        moment_two = 0.5 * moment_two + 0.5 * clipped * clipped
        if index == 2 or index == 4:
            results = results + [moment_one, moment_two, clipped]
        else:
            master = master - RATE * (
                moment_one / correction / (jnp.sqrt(moment_two / correction) + TINY)
                + DECAY * master
            )
            results = results + [moment_one, moment_two, master]
    return (
        total_loss,
        grad_norm,
        counts,
        results[0],
        results[1],
        results[2],
        results[3],
        results[4],
        results[5],
        results[6],
        results[7],
        results[8],
        results[9],
        results[10],
        results[11],
        results[12],
        results[13],
        results[14],
    )


def solution(mesh):
    in_specs = (
        P(None, ("wide", "narrow"), None, None),
        P(None, ("wide", "narrow")),
        P(None, ("wide", "narrow")),
        P(None, ("wide", "narrow")),
        P(),
        P(("wide", "narrow"), None),
        P(("wide", "narrow"), None),
        P(("wide", "narrow"), None),
        P(("wide", "narrow"), None),
        P(("wide", "narrow"), None),
        P(("wide", "narrow"), None),
        P(("wide", "narrow"), None),
        P(("wide", "narrow"), None),
        P(("wide", "narrow"), None),
        P(("wide", "narrow"), None),
        P(("wide", "narrow"), None),
        P(("wide", "narrow"), None),
        P(("wide", "narrow"), None),
        P(("wide", "narrow"), None),
        P(("wide", "narrow"), None),
    )
    out_specs = (
        P(),
        P(),
        P(),
        P(("wide", "narrow"), None),
        P(("wide", "narrow"), None),
        P(("wide", "narrow"), None),
        P(("wide", "narrow"), None),
        P(("wide", "narrow"), None),
        P(("wide", "narrow"), None),
        P(("wide", "narrow"), None),
        P(("wide", "narrow"), None),
        P(("wide", "narrow"), None),
        P(("wide", "narrow"), None),
        P(("wide", "narrow"), None),
        P(("wide", "narrow"), None),
        P(("wide", "narrow"), None),
        P(("wide", "narrow"), None),
        P(("wide", "narrow"), None),
    )
    return jax.shard_map(
        on_device, mesh=mesh, in_specs=in_specs, out_specs=out_specs, check_vma=False
    )
```

time: 1600 us -> 914 us (0.57)
  blocking collectives: 560 us -> 0 us
  waiting for transfers between devices: 464 us -> 229 us
  starting transfers between devices: 5.34 us -> 181 us
  matrix products: 327 us -> 222 us
  other arithmetic: 90.6 us -> 135 us
    all_to_all x1 -> x0, blocking collectives: 297 us -> none  [reduce_owner(): lax.all_to_all(sectioned.astype(jnp.bfloat16), 'narrow', split_axis=2, co...]
    ppermute x0 -> x156, waiting for transfers between devices: none -> 229 us  [exchange(): return lax.ppermute(values, AXES, [(i, i ^ offset) for i in range(total)])]
    all_to_all x1 -> x0, waiting for transfers between devices: 221 us -> none  [reduce_owner(): lax.all_to_all(partial_rows.astype(jnp.bfloat16), 'wide', split_axis=1, c...]
    ppermute x0 -> x156, starting transfers between devices: none -> 181 us  [exchange(): return lax.ppermute(values, AXES, [(i, i ^ offset) for i in range(total)])]
    all_gather x2 -> x0, blocking collectives: 133 us -> none  [the longest x1 66.7 us: forward_blocks(): lax.all_gather(shards_low[1], ('wide', 'narrow'), axis=0, tiled=True)]
    all_gather x4 -> x0, waiting for transfers between devices: 132 us -> none  [the longest x1 132 us: forward_blocks(): lax.all_gather(shards_low[0], ('wide', 'narrow'), axis=0, tiled=True)]
    psum x2 -> x0, blocking collectives: 130 us -> none  [the longest x1 88.4 us: on_device(): square, total_loss = lax.psum((square, loss_local), ('wide', 'narrow'))]
    unnamed x6 -> x0, waiting for transfers between devices: 111 us -> none
  transfers between devices with their start and end apart: 6 -> 156, of which waited for: 3 -> 61; matrix products, arithmetic and copies ran while one was open for 8% -> 27% of each run, Pallas kernels for 0% -> 0%
where the time goes in v1:
time: 914 us; the launch traced here: 903 us
  waiting for transfers between devices  229 us (25%)
  matrix products  222 us (24%)
  starting transfers between devices  181 us (20%)
  other arithmetic  135 us (15%)
  local copies, waits for them, and re-layouts  124 us (14%)
  between operations  11.7 us (1%)
    ppermute x156, waiting for transfers between devices, exchange(): return lax.ppermute(values, AXES, [(i, i ^ offset) for i in range(total)])  229 us
    ppermute x156, starting transfers between devices, exchange(): return lax.ppermute(values, AXES, [(i, i ^ offset) for i in range(total)])  181 us
    select_n x88, other arithmetic, in_place(): stacked = jnp.where(mine & bit != 0, swapped, stacked)  42.7 us
    unnamed x324, local copies, waits for them, and re-layouts  39.9 us
    dot_general x9, matrix products, right_dot(): lax.dot_general(first_op, second_op, (((1,), (1,)), ((), ())), preferred_...  38.8 us
    dot_general x9, matrix products, left_dot(): lax.dot_general(first_op, second_op, (((0,), (0,)), ((), ())), preferred_...  36 us
    dot_general x10, matrix products, matmul(): return jnp.dot(first_op, second_op, preferred_element_type=jnp.float32)  34.7 us
    convert_element_type x6, local copies, waits for them, and re-layouts, lowered(): return values.astype(jnp.bfloat16)  28.6 us
  transfers between devices with their start and end apart: 156, of which 61 were waited for; matrix products, arithmetic and copies ran while one was open for 27% of the time, Pallas kernels for 0%

profile of v1, /device:TPU:0, one launch (start us, length us, event | category | flops | bytes accessed | tf_op | source)
XLA Modules:
  0.0 903.0 jit_solution(13639280023858556989)
XLA Ops:
  60.9 9.6 %collective-permute-done.14 = bf16[32,1024]{1,0:T(8,128)(2,1)S(1)} collective-permute-done((bf16[32,1024]{1,0:T(8,128)(2,1)S(1)}, bf16[32,1024]{1,0:T(8,128)(2,1)S(1)}, u32[]{:S(2)}, u32[]{:S(2)}) %collective-permute-start.14) | collective-permute-done | bytes 65568 | tf_op jit(solution)/shard_map/ppermute | solution.py:75
  122.5 9.4 %collective-permute-done.21 = bf16[4,32,1024]{2,1,0:T(8,128)(2,1)S(1)} collective-permute-done((bf16[4,32,1024]{2,1,0:T(8,128)(2,1)S(1)}, bf16[4,32,1024]{2,1,0:T(8,128)(2,1)S(1)}, u32[]{:S(2)}, u32[]{:S(2)}) %collective-permute-start.21) | collective-permute-done | bytes 262176 | tf_op jit(solution)/shard_map/ppermute | solution.py:75
  139.1 7.6 collective-permute-done.15
  175.8 7.4 collective-permute-done.34
  187.4 7.0 collective-permute-done.46
  292.4 9.3 %convert_bitcast_fusion = bf16[128,8,24,128]{3,1,2,0:T(8,128)(2,1)} fusion(bf16[1024,3072]{1,0:T(8,128)(2,1)S(1)} %bitcast.832, f32[1024,1024]{1,0:T(8,128)S(1)} %get-tuple-element.359, f32[1024]{0:T(1024)S(1)} %get-tuple-element.163, f32[1024]{0:T(1024)S(1)} %get-tuple-element.164, f32[1024]{0:T(1024)S(1)} %fusion.208, f32[1024]{0:T(1024)S(1)} %broadcast_multiply_fusion.3), kind=kOutput, calls=%fused_computation.29 | convolution fusion | flops 6450839552 | bytes 16793600 | tf_op jit(solution)/shard_map/dot_general | solution.py:22
  312.4 11.1 %fusion.79 = f32[2,8,512,512]{2,3,1,0:T(8,128)} fusion(bf16[2,512,1,8,128]{4,3,2,1,0:T(8,128)(2,1)} %get-tuple-element.204, bf16[2,512,1,8,128]{4,3,2,1,0:T(8,128)(2,1)} %get-tuple-element.202), kind=kOutput, calls=%fused_computation.155 | convolution fusion | flops 1073741824 | bytes 20971520 | tf_op jit(solution)/shard_map/blhe,bmhe->bhlm/dot_general | solution.py:243
  323.5 19.3 %fusion.258 = (f32[2,8,512]{2,1,0:T(8,128)S(1)}, f32[2,8,512,512]{2,3,1,0:T(8,128)}) fusion(f32[2,8,512,512]{2,3,1,0:T(8,128)} %fusion.79), kind=kOutput, calls=%fused_computation.671 | output fusion | flops 16777728 | bytes 33587200 | tf_op jit(solution)/shard_map/sub | solution.py:246
  342.8 8.4 convert_bitcast_fusion.3
  441.6 10.3 %fusion.46 = bf16[2,512,1,8,128]{1,4,3,0,2:T(8,128)(2,1)} fusion(bf16[2,512,8,128]{1,3,2,0:T(8,128)(2,1)S(1)} %copy.814, f32[2,8,512,512]{2,3,1,0:T(8,128)} %get-tuple-element.361, f32[2,8,512]{2,1,0:T(8,128)S(1)} %get-tuple-element.360), kind=kOutput, calls=%fused_computation.98 | convolution fusion | flops 1082130432 | bytes 21004288 | tf_op jit(solution)/shard_map/bhlm,blhe->bmhe/dot_general | solution.py:298
  451.9 8.2 fusion.66
  460.1 25.3 %fusion.49 = bf16[2,512,1,8,128]{1,4,3,0,2:T(8,128)(2,1)} fusion(f32[2,8,512,512]{2,3,1,0:T(8,128)} %fusion.66, bf16[2,512,1,8,128]{4,3,2,1,0:T(8,128)(2,1)} %get-tuple-element.202, f32[2,8,512,512]{2,3,1,0:T(8,128)} %get-tuple-element.361, f32[2,8,512]{2,1,0:T(8,128)S(1)} %get-tuple-element.360), kind=kOutput, calls=%fused_computation.99 | convolution fusion | flops 1103110656 | bytes 37781504 | tf_op jit(solution)/shard_map/bhlm,bmhe->blhe/dot_general | solution.py:302
  485.4 24.0 %fusion.52 = bf16[2,512,1,8,128]{1,4,3,0,2:T(8,128)(2,1)} fusion(f32[2,8,512,512]{2,3,1,0:T(8,128)} %fusion.66, bf16[2,512,1,8,128]{4,3,2,1,0:T(8,128)(2,1)S(1)} %copy-done.18, f32[2,8,512,512]{2,3,1,0:T(8,128)} %get-tuple-element.361, f32[2,8,512]{2,1,0:T(8,128)S(1)} %get-tuple-element.360), kind=kOutput, calls=%fused_computation.100 | convolution fusion | flops 1103110656 | bytes 37781504 | tf_op jit(solution)/shard_map/bhlm,blhe->bmhe/dot_general | solution.py:305
  515.6 9.1 %copy.816 = bf16[2,512,3,8,128]{4,3,2,1,0:T(8,128)(2,1)} copy(bf16[2,512,3,8,128]{1,4,3,0,2:T(8,128)(2,1)} %maximum_convert_fusion) | data formatting | bytes 12582912 | tf_op jit(solution)/shard_map/convert_element_type | solution.py:18
  524.7 10.4 %convert_element_type.741 = bf16[1024,3072]{1,0:T(8,128)(2,1)} reshape(bf16[2,512,3,8,128]{4,3,2,1,0:T(8,128)(2,1)} %copy.816) | data formatting | bytes 12582912 | tf_op jit(solution)/shard_map/convert_element_type | solution.py:18
  535.1 12.4 %multiply_reduce_fusion.3 = (bf16[1024]{0:T(1024)(128)(2,1)S(1)}, f32[1024]{0:T(1024)S(1)}, bf16[1024]{0:T(1024)(128)(2,1)S(1)}, f32[1024,1024]{1,0:T(8,128)S(1)}) fusion(f32[1024,1024]{1,0:T(8,128)} %copy-done.6, f32[1024]{0:T(1024)S(1)} %copy-done.109, f32[1024]{0:T(1024)S(1)} %copy-done.96, f32[1024]{0:T(1024)S(1)} %copy-done.107, ...), kind=kOutput, calls=%fused_computation.57 | convolution fusion | flops 6450836480 | bytes 20992000 | tf_op jit(solution)/shard_map/dot_general | solution.py:32
  547.6 9.2 %convolution_convert_fusion = bf16[1024,3072]{1,0:T(8,128)(2,1)} fusion(bf16[1024,3072]{1,0:T(8,128)(2,1)S(1)} %copy-done.20, f32[1024,1024]{1,0:T(8,128)S(1)} %copy-done.7, f32[1024]{0:T(1024)S(1)} %copy-done.126, f32[1024]{0:T(1024)S(1)} %copy-done.107, f32[1024]{0:T(1024)S(1)} %copy-done.109, f32[1024]{0:T(1024)S(1)} %copy-done.96), kind=kOutput, calls=%fused_computation.36 | convolution fusion | flops 6450839552 | bytes 16793600 | tf_op jit(solution)/shard_map/dot_general | solution.py:26
  713.2 10.2 %collective-permute-done.105 = bf16[4,2,32,1024]{3,2,0,1:T(8,128)(2,1)S(1)} collective-permute-done((bf16[4,2,32,1024]{3,2,0,1:T(8,128)(2,1)S(1)}, bf16[4,2,32,1024]{3,2,0,1:T(8,128)(2,1)S(1)}, u32[]{:S(2)}, u32[]{:S(2)}) %collective-permute-start.105) | collective-permute-done | bytes 524320 | tf_op jit(solution)/shard_map/ppermute | solution.py:75
  725.4 9.2 %collective-permute-done.117 = bf16[4,2,32,1024]{3,2,0,1:T(8,128)(2,1)S(1)} collective-permute-done((bf16[4,2,32,1024]{3,2,0,1:T(8,128)(2,1)S(1)}, bf16[4,2,32,1024]{3,2,0,1:T(8,128)(2,1)S(1)}, u32[]{:S(2)}, u32[]{:S(2)}) %collective-permute-start.117) | collective-permute-done | bytes 524320 | tf_op jit(solution)/shard_map/ppermute | solution.py:75
  736.7 9.1 %collective-permute-done.93 = bf16[4,2,32,1024]{3,2,0,1:T(8,128)(2,1)S(1)} collective-permute-done((bf16[4,2,32,1024]{3,2,0,1:T(8,128)(2,1)S(1)}, bf16[4,2,32,1024]{3,2,0,1:T(8,128)(2,1)S(1)}, u32[]{:S(2)}, u32[]{:S(2)}) %collective-permute-start.93) | collective-permute-done | bytes 524320 | tf_op jit(solution)/shard_map/ppermute | solution.py:75
  748.4 8.7 collective-permute-done.87
  767.2 9.3 %collective-permute-done.88 = bf16[4,32,1024]{2,1,0:T(8,128)(2,1)S(1)} collective-permute-done((bf16[4,32,1024]{2,1,0:T(8,128)(2,1)S(1)}, bf16[4,32,1024]{2,1,0:T(8,128)(2,1)S(1)}, u32[]{:S(2)}, u32[]{:S(2)}) %collective-permute-start.88) | collective-permute-done | bytes 262176 | tf_op jit(solution)/shard_map/ppermute | solution.py:75
  781.6 27.0 %collective-permute-done.111 = bf16[4,2,32,3072]{3,2,0,1:T(8,128)(2,1)S(1)} collective-permute-done((bf16[4,2,32,3072]{3,2,0,1:T(8,128)(2,1)S(1)}, bf16[4,2,32,3072]{3,2,0,1:T(8,128)(2,1)S(1)}, u32[]{:S(2)}, u32[]{:S(2)}) %collective-permute-start.111) | collective-permute-done | bytes 1572896 | tf_op jit(solution)/shard_map/ppermute | solution.py:75
  847.0 9.8 %collective-permute-done.114 = bf16[32,3072]{1,0:T(8,128)(2,1)S(1)} collective-permute-done((bf16[32,3072]{1,0:T(8,128)(2,1)S(1)}, bf16[32,3072]{1,0:T(8,128)(2,1)S(1)}, u32[]{:S(2)}, u32[]{:S(2)}) %collective-permute-start.114) | collective-permute-done | bytes 196640 | tf_op jit(solution)/shard_map/ppermute | solution.py:75
  (992 shorter events, 610.1 us)
Async XLA Ops:
  55.3 60.4 %collective-permute-start.37 = (bf16[32,3072]{1,0:T(8,128)(2,1)S(1)}, bf16[32,3072]{1,0:T(8,128)(2,1)S(1)}, u32[]{:S(2)}, u32[]{:S(2)}) collective-permute-start(bf16[32,3072]{1,0:T(8,128)(2,1)S(1)} %get-tuple-element.250), channel_id=1, source_target_pairs={{0,24},{1,25},{2,26},{3,27},{4,28},{5,29},{6,30},{7,31},{8,16},{9,... | collective-permute-start | bytes 589832 | tf_op jit(solution)/shard_map/ppermute | solution.py:75
  60.7 55.5 %collective-permute-start.38 = (bf16[32,3072]{1,0:T(8,128)(2,1)S(1)}, bf16[32,3072]{1,0:T(8,128)(2,1)S(1)}, u32[]{:S(2)}, u32[]{:S(2)}) collective-permute-start(bf16[32,3072]{1,0:T(8,128)(2,1)S(1)} %get-tuple-element.250), channel_id=1, source_target_pairs={{0,16},{1,17},{2,18},{3,19},{4,20},{5,21},{6,22},{7,23},{8,24},{9,... | collective-permute-start | bytes 589832 | tf_op jit(solution)/shard_map/ppermute | solution.py:75
  115.7 33.1 %collective-permute-start.27 = (bf16[4,32,1024]{2,1,0:T(8,128)(2,1)S(1)}, bf16[4,32,1024]{2,1,0:T(8,128)(2,1)S(1)}, u32[]{:S(2)}, u32[]{:S(2)}) collective-permute-start(bf16[4,32,1024]{2,1,0:T(8,128)(2,1)S(1)} %maximum_select_fusion.61), channel_id=1, source_target_pairs={{0,4},{1,5},{2,6},{3,7},{4,0},{5,1},{6,2},{7,3},{8,12},{9,13},{10,... | collective-permute-start | bytes 786440 | tf_op jit(solution)/shard_map/ppermute | solution.py:75
  137.1 80.8 %collective-permute-start.39 = (bf16[4,32,3072]{2,1,0:T(8,128)(2,1)S(1)}, bf16[4,32,3072]{2,1,0:T(8,128)(2,1)S(1)}, u32[]{:S(2)}, u32[]{:S(2)}) collective-permute-start(bf16[4,32,3072]{2,1,0:T(8,128)(2,1)S(1)} %maximum_select_fusion.34), channel_id=1, source_target_pairs={{0,4},{1,5},{2,6},{3,7},{4,0},{5,1},{6,2},{7,3},{8,12},{9,13},{10,... | collective-permute-start | bytes 2359304 | tf_op jit(solution)/shard_map/ppermute | solution.py:75
  155.1 28.1 %collective-permute-start.34 = (bf16[4,2,32,1024]{3,2,0,1:T(8,128)(2,1)S(1)}, bf16[4,2,32,1024]{3,2,0,1:T(8,128)(2,1)S(1)}, u32[]{:S(2)}, u32[]{:S(2)}) collective-permute-start(bf16[4,2,32,1024]{3,2,0,1:T(8,128)(2,1)S(1)} %maximum_select_fusion.43), channel_id=1, source_target_pairs={{0,4},{1,5},{2,6},{3,7},{4,0},{5,1},{6,2},{7,3},{8,12},{9,13},{10,... | collective-permute-start | bytes 1572872 | tf_op jit(solution)/shard_map/ppermute | solution.py:75
  157.4 37.1 %collective-permute-start.46 = (bf16[4,2,32,1024]{3,2,0,1:T(8,128)(2,1)S(1)}, bf16[4,2,32,1024]{3,2,0,1:T(8,128)(2,1)S(1)}, u32[]{:S(2)}, u32[]{:S(2)}) collective-permute-start(bf16[4,2,32,1024]{3,2,0,1:T(8,128)(2,1)S(1)} %maximum_select_fusion.45), channel_id=1, source_target_pairs={{0,4},{1,5},{2,6},{3,7},{4,0},{5,1},{6,2},{7,3},{8,12},{9,13},{10,... | collective-permute-start | bytes 1572872 | tf_op jit(solution)/shard_map/ppermute | solution.py:75
  164.6 33.7 %collective-permute-start.52 = (bf16[4,2,32,1024]{3,2,0,1:T(8,128)(2,1)S(1)}, bf16[4,2,32,1024]{3,2,0,1:T(8,128)(2,1)S(1)}, u32[]{:S(2)}, u32[]{:S(2)}) collective-permute-start(bf16[4,2,32,1024]{3,2,0,1:T(8,128)(2,1)S(1)} %maximum_select_fusion.47), channel_id=1, source_target_pairs={{0,1},{1,0},{2,3},{3,2},{4,5},{5,4},{6,7},{7,6},{8,9},{9,8},{10,11... | collective-permute-start | bytes 1572872 | tf_op jit(solution)/shard_map/ppermute | solution.py:75
  172.0 37.3 %collective-permute-start.58 = (bf16[4,2,32,1024]{3,2,0,1:T(8,128)(2,1)S(1)}, bf16[4,2,32,1024]{3,2,0,1:T(8,128)(2,1)S(1)}, u32[]{:S(2)}, u32[]{:S(2)}) collective-permute-start(bf16[4,2,32,1024]{3,2,0,1:T(8,128)(2,1)S(1)} %maximum_select_fusion.49), channel_id=1, source_target_pairs={{0,4},{1,5},{2,6},{3,7},{4,0},{5,1},{6,2},{7,3},{8,12},{9,13},{10,... | collective-permute-start | bytes 1572872 | tf_op jit(solution)/shard_map/ppermute | solution.py:75
  232.2 156.1 %collective-permute-start.75 = (bf16[4,2,2,32,1000]{4,3,0,1,2:T(8,128)(2,1)}, bf16[4,2,2,32,1000]{4,3,0,1,2:T(8,128)(2,1)}, u32[]{:S(2)}, u32[]{:S(2)}) collective-permute-start(bf16[4,2,2,32,1000]{4,3,0,1,2:T(8,128)(2,1)} %maximum_select_fusion.29), channel_id=1, source_target_pairs={{0,2},{1,3},{2,0},{3,1},{4,6},{5,7},{6,4},{7,5},{8,10},{9,11},{10,... | collective-permute-start | bytes 3072008 | tf_op jit(solution)/shard_map/ppermute | solution.py:75
  240.7 37.1 %collective-permute-start.40 = (bf16[4,2,32,3072]{3,2,0,1:T(8,128)(2,1)}, bf16[4,2,32,3072]{3,2,0,1:T(8,128)(2,1)}, u32[]{:S(2)}, u32[]{:S(2)}) collective-permute-start(bf16[4,2,32,3072]{3,2,0,1:T(8,128)(2,1)} %maximum_select_fusion.12), channel_id=1, source_target_pairs={{0,1},{1,0},{2,3},{3,2},{4,5},{5,4},{6,7},{7,6},{8,9},{9,8},{10,11... | collective-permute-start | bytes 4718600 | tf_op jit(solution)/shard_map/ppermute | solution.py:75
  604.0 76.8 %collective-permute-start.122 = (bf16[4,2,2,32,1024]{4,3,0,2,1:T(8,128)(2,1)}, bf16[4,2,2,32,1024]{4,3,0,2,1:T(8,128)(2,1)}, u32[]{:S(2)}, u32[]{:S(2)}) collective-permute-start(bf16[4,2,2,32,1024]{4,3,0,2,1:T(8,128)(2,1)} %bitcast.815), channel_id=1, source_target_pairs={{0,2},{1,3},{2,0},{3,1},{4,6},{5,7},{6,4},{7,5},{8,10},{9,11},{10,... | collective-permute-start | bytes 3145736 | tf_op jit(solution)/shard_map/ppermute | solution.py:75
  604.0 78.9 %collective-permute-start.128 = (bf16[4,2,2,32,1024]{4,3,0,1,2:T(8,128)(2,1)}, bf16[4,2,2,32,1024]{4,3,0,1,2:T(8,128)(2,1)}, u32[]{:S(2)}, u32[]{:S(2)}) collective-permute-start(bf16[4,2,2,32,1024]{4,3,0,1,2:T(8,128)(2,1)} %bitcast.814), channel_id=1, source_target_pairs={{0,2},{1,3},{2,0},{3,1},{4,6},{5,7},{6,4},{7,5},{8,10},{9,11},{10,... | collective-permute-start | bytes 3145736 | tf_op jit(solution)/shard_map/ppermute | solution.py:75
  680.6 84.6 %collective-permute-start.110 = (bf16[4,2,2,32,3072]{4,3,0,2,1:T(8,128)(2,1)S(1)}, bf16[4,2,2,32,3072]{4,3,0,2,1:T(8,128)(2,1)S(1)}, u32[]{:S(2)}, u32[]{:S(2)}) collective-permute-start(bf16[4,2,2,32,3072]{4,3,0,2,1:T(8,128)(2,1)S(1)} %bitcast.855), channel_id=1, source_target_pairs={{0,2},{1,3},{2,0},{3,1},{4,6},{5,7},{6,4},{7,5},{8,10},{9,11},{10,... | collective-permute-start | bytes 9437192 | tf_op jit(solution)/shard_map/ppermute | solution.py:75
  701.9 32.7 %collective-permute-start.117 = (bf16[4,2,32,1024]{3,2,0,1:T(8,128)(2,1)S(1)}, bf16[4,2,32,1024]{3,2,0,1:T(8,128)(2,1)S(1)}, u32[]{:S(2)}, u32[]{:S(2)}) collective-permute-start(bf16[4,2,32,1024]{3,2,0,1:T(8,128)(2,1)S(1)} %dynamic-slice_bitcast_fusion.6), channel_id=1, source_target_pairs={{0,1},{1,0},{2,3},{3,2},{4,5},{5,4},{6,7},{7,6},{8,9},{9,8},{10,11... | collective-permute-start | bytes 1572872 | tf_op jit(solution)/shard_map/ppermute | solution.py:75
  704.4 41.4 %collective-permute-start.93 = (bf16[4,2,32,1024]{3,2,0,1:T(8,128)(2,1)S(1)}, bf16[4,2,32,1024]{3,2,0,1:T(8,128)(2,1)S(1)}, u32[]{:S(2)}, u32[]{:S(2)}) collective-permute-start(bf16[4,2,32,1024]{3,2,0,1:T(8,128)(2,1)S(1)} %dynamic-slice_bitcast_fusion.9), channel_id=1, source_target_pairs={{0,1},{1,0},{2,3},{3,2},{4,5},{5,4},{6,7},{7,6},{8,9},{9,8},{10,11... | collective-permute-start | bytes 1572872 | tf_op jit(solution)/shard_map/ppermute | solution.py:75
  712.1 34.7 %collective-permute-start.99 = (bf16[4,2,32,1024]{3,2,0,1:T(8,128)(2,1)S(1)}, bf16[4,2,32,1024]{3,2,0,1:T(8,128)(2,1)S(1)}, u32[]{:S(2)}, u32[]{:S(2)}) collective-permute-start(bf16[4,2,32,1024]{3,2,0,1:T(8,128)(2,1)S(1)} %dynamic-slice_bitcast_fusion.8), channel_id=1, source_target_pairs={{0,4},{1,5},{2,6},{3,7},{4,0},{5,1},{6,2},{7,3},{8,12},{9,13},{10,... | collective-permute-start | bytes 1572872 | tf_op jit(solution)/shard_map/ppermute | solution.py:75
  723.4 33.7 %collective-permute-start.87 = (bf16[4,2,32,1024]{3,2,0,1:T(8,128)(2,1)S(1)}, bf16[4,2,32,1024]{3,2,0,1:T(8,128)(2,1)S(1)}, u32[]{:S(2)}, u32[]{:S(2)}) collective-permute-start(bf16[4,2,32,1024]{3,2,0,1:T(8,128)(2,1)S(1)} %dynamic-slice_bitcast_fusion.10), channel_id=1, source_target_pairs={{0,1},{1,0},{2,3},{3,2},{4,5},{5,4},{6,7},{7,6},{8,9},{9,8},{10,11... | collective-permute-start | bytes 1572872 | tf_op jit(solution)/shard_map/ppermute | solution.py:75
  734.6 26.4 %collective-permute-start.124 = (bf16[4,32,1024]{2,1,0:T(8,128)(2,1)S(1)}, bf16[4,32,1024]{2,1,0:T(8,128)(2,1)S(1)}, u32[]{:S(2)}, u32[]{:S(2)}) collective-permute-start(bf16[4,32,1024]{2,1,0:T(8,128)(2,1)S(1)} %dynamic-slice_bitcast_fusion.14), channel_id=1, source_target_pairs={{0,1},{1,0},{2,3},{3,2},{4,5},{5,4},{6,7},{7,6},{8,9},{9,8},{10,11... | collective-permute-start | bytes 786440 | tf_op jit(solution)/shard_map/ppermute | solution.py:75
  766.5 42.1 %collective-permute-start.111 = (bf16[4,2,32,3072]{3,2,0,1:T(8,128)(2,1)S(1)}, bf16[4,2,32,3072]{3,2,0,1:T(8,128)(2,1)S(1)}, u32[]{:S(2)}, u32[]{:S(2)}) collective-permute-start(bf16[4,2,32,3072]{3,2,0,1:T(8,128)(2,1)S(1)} %dynamic-slice_bitcast_fusion), channel_id=1, source_target_pairs={{0,4},{1,5},{2,6},{3,7},{4,0},{5,1},{6,2},{7,3},{8,12},{9,13},{10,... | collective-permute-start | bytes 4718600 | tf_op jit(solution)/shard_map/ppermute | solution.py:75
  776.4 87.5 %collective-permute-start.125 = (bf16[32,1024]{1,0:T(8,128)(2,1)S(1)}, bf16[32,1024]{1,0:T(8,128)(2,1)S(1)}, u32[]{:S(2)}, u32[]{:S(2)}) collective-permute-start(bf16[32,1024]{1,0:T(8,128)(2,1)S(1)} %get-tuple-element.267), channel_id=1, source_target_pairs={{0,8},{1,9},{2,10},{3,11},{4,12},{5,13},{6,14},{7,15},{8,0},{9,1},... | collective-permute-start | bytes 196616 | tf_op jit(solution)/shard_map/ppermute | solution.py:75
  777.6 33.6 %collective-permute-start.89 = (bf16[32,1024]{1,0:T(8,128)(2,1)S(1)}, bf16[32,1024]{1,0:T(8,128)(2,1)S(1)}, u32[]{:S(2)}, u32[]{:S(2)}) collective-permute-start(bf16[32,1024]{1,0:T(8,128)(2,1)S(1)} %get-tuple-element.282), channel_id=1, source_target_pairs={{0,8},{1,9},{2,10},{3,11},{4,12},{5,13},{6,14},{7,15},{8,0},{9,1},... | collective-permute-start | bytes 196616 | tf_op jit(solution)/shard_map/ppermute | solution.py:75
  778.8 34.0 %collective-permute-start.91 = (bf16[32,1024]{1,0:T(8,128)(2,1)S(1)}, bf16[32,1024]{1,0:T(8,128)(2,1)S(1)}, u32[]{:S(2)}, u32[]{:S(2)}) collective-permute-start(bf16[32,1024]{1,0:T(8,128)(2,1)S(1)} %get-tuple-element.283), channel_id=1, source_target_pairs={{0,24},{1,25},{2,26},{3,27},{4,28},{5,29},{6,30},{7,31},{8,16},{9,... | collective-permute-start | bytes 196616 | tf_op jit(solution)/shard_map/ppermute | solution.py:75
  780.7 33.4 %collective-permute-start.90 = (bf16[32,1024]{1,0:T(8,128)(2,1)S(1)}, bf16[32,1024]{1,0:T(8,128)(2,1)S(1)}, u32[]{:S(2)}, u32[]{:S(2)}) collective-permute-start(bf16[32,1024]{1,0:T(8,128)(2,1)S(1)} %get-tuple-element.284), channel_id=1, source_target_pairs={{0,16},{1,17},{2,18},{3,19},{4,20},{5,21},{6,22},{7,23},{8,24},{9,... | collective-permute-start | bytes 196616 | tf_op jit(solution)/shard_map/ppermute | solution.py:75
  823.1 40.9 %collective-permute-start.127 = (bf16[32,1024]{1,0:T(8,128)(2,1)S(1)}, bf16[32,1024]{1,0:T(8,128)(2,1)S(1)}, u32[]{:S(2)}, u32[]{:S(2)}) collective-permute-start(bf16[32,1024]{1,0:T(8,128)(2,1)S(1)} %get-tuple-element.268), channel_id=1, source_target_pairs={{0,24},{1,25},{2,26},{3,27},{4,28},{5,29},{6,30},{7,31},{8,16},{9,... | collective-permute-start | bytes 196616 | tf_op jit(solution)/shard_map/ppermute | solution.py:75
  (284 other events, 3045.9 us)

commit v2 on v1

v2 whole, which is shorter than its diff:
```python
import functools

import jax
import jax.numpy as jnp
from jax import lax
from jax.experimental import pallas as pl
from jax.experimental.pallas import tpu as pltpu
from jax.sharding import PartitionSpec as P

HEADS = 8
AXES = ("wide", "narrow")

EPSILON = 1e-05
RATE = 0.03
DECAY = 0.1
TINY = 1e-08
THRESH = 0.01
BEND = 0.044715
MARKS = 128
SLOPE = 0.7978845608028654
VMEM = pltpu.VMEM
MIB = 1 << 20


def lowered(values):
    return values.astype(jnp.bfloat16)


def dot_nn(first_op, second_op):
    return jnp.dot(first_op, second_op, preferred_element_type=jnp.float32)


def dot_tn(first_op, second_op):
    return lax.dot_general(
        first_op, second_op, (((0,), (0,)), ((), ())), preferred_element_type=jnp.float32
    )


def dot_nt(first_op, second_op):
    return lax.dot_general(
        first_op, second_op, (((1,), (1,)), ((), ())), preferred_element_type=jnp.float32
    )


def standard(inputs):
    center = inputs - jnp.mean(inputs, axis=-1, keepdims=True)
    scale = lax.rsqrt(jnp.mean(center * center, axis=-1, keepdims=True) + EPSILON)
    return center * scale, scale


def layer_norm(inputs, scales, column):
    return standard(inputs)[0] * scales[column : column + 1, :] + scales[column + 1 : column + 2, :]


def norm_back(inputs, scales, column, upstream):
    unit, scale = standard(inputs)
    gain = jnp.sum(upstream * unit, axis=0, keepdims=True)
    bias = jnp.sum(upstream, axis=0, keepdims=True)
    inner = upstream * scales[column : column + 1, :]
    back = scale * (
        inner
        - jnp.mean(inner, axis=-1, keepdims=True)
        - unit * jnp.mean(inner * unit, axis=-1, keepdims=True)
    )
    return back, gain, bias


def gelu_both(values):
    square = values * values
    bent = jnp.tanh(SLOPE * values * (1.0 + BEND * square))
    half = 0.5 * (1.0 + bent)
    steep = half + 0.5 * values * (1.0 - bent * bent) * SLOPE * (1.0 + 3.0 * BEND * square)
    return values * half, steep


def softmax(scores):
    raised = jnp.exp(scores - jnp.max(scores, axis=-1, keepdims=True))
    return raised * (1.0 / jnp.sum(raised, axis=-1, keepdims=True))


def softmax_back(attend, upstream):
    return attend * (upstream - jnp.sum(upstream * attend, axis=-1, keepdims=True))


class Half:
    def __init__(self, arrays, offsets, rows):
        self.arrays = arrays
        self.offsets = offsets
        self.rows = rows

    def start(self, refs, me, target, sem, column, stride=None, shift=0):
        width = target.shape[1]
        if self.offsets is None:
            pltpu.make_async_copy(refs[0].at[0, :, column : column + width], target, sem).start()
            return
        stride = self.rows if stride is None else stride
        for ref, offsets in zip(refs, self.offsets):
            for group, offset in enumerate(offsets):
                spot = pl.multiple_of((me ^ offset) * stride + shift, self.rows)
                pltpu.make_async_copy(
                    ref.at[group, :, column : column + width],
                    target.at[pl.ds(spot, self.rows), :],
                    sem,
                ).start()


def arrived(target, sem):
    pltpu.make_async_copy(target, target, sem).wait()


def cost(micros):
    return pl.CostEstimate(flops=int(micros * 1.1e9), bytes_accessed=1 << 20, transcendentals=0)


def params(mib, dims=1):
    return pltpu.CompilerParams(
        vmem_limit_bytes=mib * MIB, dimension_semantics=("arbitrary",) * dims
    )


def launch(kernel, after, operands, in_specs, **rest):
    extra = len(after)

    def inner(*refs):
        kernel(*refs[: len(operands)], *refs[len(operands) + extra :])

    return pl.pallas_call(inner, in_specs=list(in_specs) + [ANY] * extra, **rest)(*operands, *after)


ANY = pl.BlockSpec(memory_space=pl.ANY)
SMEM = pl.BlockSpec(memory_space=pltpu.SMEM)


def whole(shape):
    return pl.BlockSpec(shape, lambda *ids: (0,) * len(shape))


def by_crop(shape, rank=1):
    return pl.BlockSpec(shape, lambda m, *ids: (m,) + (0,) * (len(shape) - 1))


def shaped(shape, dtype):
    return jax.ShapeDtypeStruct(shape, dtype)


def run_cross_forward(me, pictures, small, kv, first, second, width, tokens, after=()):
    micro, spots, channels = pictures.shape
    parts = (small, kv, first, second)
    counts = [len(part[0].arrays) for part in parts]
    small_columns = tokens + 128

    def kernel(me_ref, pic_ref, *refs):
        groups = []
        at = 0
        for count in counts:
            groups.append(refs[at : at + count])
            at += count
        latent_ref, blended_ref, attend_ref, pair_ref, initial_ref, hidden_ref, query_ref, scale_ref = refs[at : at + 8]
        small_s, kv_s, first_s, second_s, sems = refs[at + 8 :]
        me_now = me_ref[0]
        step = pl.program_id(0)

        @pl.when(step == 0)
        def _():
            small[0].start(groups[0], me_now, small_s, sems.at[0], small[1])
            if kv[0].offsets is None:
                kv[0].start(groups[1], me_now, kv_s, sems.at[1], 0)
            else:
                rows = kv[0].rows
                kv[0].start(groups[1], me_now, kv_s, sems.at[1], kv[1], 2 * rows, 0)
                kv[0].start(groups[1], me_now, kv_s, sems.at[1], kv[1] + channels, 2 * rows, rows)
            first[0].start(groups[2], me_now, first_s, sems.at[2], first[1])
            second[0].start(groups[3], me_now, second_s, sems.at[3], second[1])
            arrived(small_s, sems.at[0])
            turned = small_s[...].astype(jnp.float32).T
            initial_ref[...] = turned[:tokens]
            scale_ref[...] = turned[tokens : tokens + 16]
            hidden_ref[...] = lowered(layer_norm(initial_ref[...], scale_ref, 0))
            arrived(first_s, sems.at[2])
            query_ref[...] = lowered(dot_nn(hidden_ref[...], first_s[...]))
            arrived(kv_s, sems.at[1])
            arrived(second_s, sems.at[3])

        pair_ref[0] = lowered(dot_nt(pic_ref[0], kv_s[...]))
        scores = dot_nt(query_ref[...], pair_ref[0, :, :width]) * width ** (-0.5)
        attend = softmax(scores)
        attend_ref[0] = attend
        blended_ref[...] = lowered(dot_nn(lowered(attend), pair_ref[0, :, width:]))
        latent_ref[...] = initial_ref[...] + dot_nn(blended_ref[...], second_s[...])

    total = micro * tokens
    return launch(
        kernel,
        after,
        [me, pictures, *[array for part in parts for array in part[0].arrays]],
        grid=(micro,),
        in_specs=[SMEM, by_crop((1, spots, channels))] + [ANY] * sum(counts),
        out_specs=[
            by_crop((tokens, width)),
            by_crop((tokens, width)),
            by_crop((1, tokens, spots)),
            by_crop((1, spots, 2 * width)),
            whole((tokens, width)),
            whole((tokens, width)),
            whole((tokens, width)),
            whole((16, width)),
        ],
        out_shape=[
            shaped((total, width), jnp.float32),
            shaped((total, width), jnp.bfloat16),
            shaped((micro, tokens, spots), jnp.float32),
            shaped((micro, spots, 2 * width), jnp.bfloat16),
            shaped((tokens, width), jnp.float32),
            shaped((tokens, width), jnp.bfloat16),
            shaped((tokens, width), jnp.bfloat16),
            shaped((16, width), jnp.float32),
        ],
        scratch_shapes=[
            VMEM((width, small_columns), jnp.bfloat16),
            VMEM((2 * width, channels), jnp.bfloat16),
            VMEM((width, width), jnp.bfloat16),
            VMEM((width, width), jnp.bfloat16),
            pltpu.SemaphoreType.DMA((4,)),
        ],
        compiler_params=params(48),
        cost_estimate=cost(18),
        name="cross_forward",
    )


def run_feed_forward(me, scales, latent, first, second, column, micro, pool, after=()):
    total, width = latent.shape
    tokens = total // micro
    parts = (first, second)
    counts = [len(part[0].arrays) for part in parts]

    def kernel(me_ref, scale_ref, latent_ref, *refs):
        first_refs, refs = refs[: counts[0]], refs[counts[0] :]
        second_refs, refs = refs[: counts[1]], refs[counts[1] :]
        out_ref, hidden_ref, active_ref, steep_ref = refs[:4]
        first_s, second_s, sems = refs[-3:]
        step = pl.program_id(0)

        @pl.when(step == 0)
        def _():
            first[0].start(first_refs, me_ref[0], first_s, sems.at[0], first[1])
            second[0].start(second_refs, me_ref[0], second_s, sems.at[1], second[1])

        hidden_ref[...] = lowered(layer_norm(latent_ref[...], scale_ref, column))

        @pl.when(step == 0)
        def _():
            arrived(first_s, sems.at[0])

        pieces = 4
        span = width // pieces
        for piece in range(pieces):
            cut = slice(piece * span, (piece + 1) * span)
            active, steep = gelu_both(dot_nn(hidden_ref[...], first_s[:, cut]))
            active_ref[:, cut] = lowered(active)
            steep_ref[:, cut] = lowered(steep)

        @pl.when(step == 0)
        def _():
            arrived(second_s, sems.at[1])

        out_ref[...] = latent_ref[...] + dot_nn(active_ref[...], second_s[...])
        if pool:
            normed = layer_norm(out_ref[...], scale_ref, 8)
            refs[4][0] = lowered(jnp.mean(normed, axis=0, keepdims=True))

    out_shape = [shaped((total, width), jnp.float32)] + [shaped((total, width), jnp.bfloat16)] * 3
    out_specs = [by_crop((tokens, width))] * 4
    if pool:
        out_shape.append(shaped((micro, 1, width), jnp.bfloat16))
        out_specs.append(by_crop((1, 1, width)))
    return launch(
        kernel,
        after,
        [me, scales, latent, *[array for part in parts for array in part[0].arrays]],
        grid=(micro,),
        in_specs=[SMEM, whole((16, width)), by_crop((tokens, width))] + [ANY] * sum(counts),
        out_specs=out_specs,
        out_shape=out_shape,
        scratch_shapes=[
            VMEM((width, width), jnp.bfloat16),
            VMEM((width, width), jnp.bfloat16),
            pltpu.SemaphoreType.DMA((2,)),
        ],
        compiler_params=params(48),
        cost_estimate=cost(16),
        name="feed_forward",
    )


def run_self_forward(me, scales, latent, query, key, value, out, micro, after=()):
    total, width = latent.shape
    tokens = total // micro
    part = width // HEADS
    pair = 2 * part
    turns = HEADS // 2
    parts = (query, key, value, out)
    counts = [len(entry[0].arrays) for entry in parts]

    def kernel(me_ref, scale_ref, latent_ref, *refs):
        groups = []
        at = 0
        for count in counts:
            groups.append(refs[at : at + count])
            at += count
        out_ref, hidden_ref, packed_ref, attend_ref, blended_ref = refs[at : at + 5]
        packed_s, out_s, sems = refs[at + 5 :]
        step, turn = pl.program_id(0), pl.program_id(1)

        @pl.when((step == 0) & (turn == 0))
        def _():
            for number in range(3):
                parts[number][0].start(
                    groups[number], me_ref[0], packed_s.at[number], sems.at[number], parts[number][1]
                )
            out[0].start(groups[3], me_ref[0], out_s, sems.at[3], out[1])

        @pl.when(turn == 0)
        def _():
            hidden_ref[...] = lowered(layer_norm(latent_ref[...], scale_ref, 4))
            for number in range(3):

                @pl.when(step == 0)
                def _():
                    arrived(packed_s.at[number], sems.at[number])

                packed_ref[:, number * width : (number + 1) * width] = lowered(
                    dot_nn(hidden_ref[...], packed_s[number])
                )

        base = pl.multiple_of(turn * pair, pair)
        queries = packed_ref[:, pl.ds(base, pair)]
        keys = packed_ref[:, pl.ds(pl.multiple_of(width + base, pair), pair)]
        values = packed_ref[:, pl.ds(pl.multiple_of(2 * width + base, pair), pair)]
        joined = []
        for head in range(2):
            cut = slice(head * part, (head + 1) * part)
            attend = softmax(dot_nt(queries[:, cut], keys[:, cut]) * part ** (-0.5))
            attend_ref[0, head] = attend
            joined.append(lowered(dot_nn(lowered(attend), values[:, cut])))
        blended_ref[:, pl.ds(base, pair)] = jnp.concatenate(joined, axis=1)

        @pl.when((step == 0) & (turn == turns - 1))
        def _():
            arrived(out_s, sems.at[3])

        @pl.when(turn == turns - 1)
        def _():
            out_ref[...] = latent_ref[...] + dot_nn(blended_ref[...], out_s[...])

    return launch(
        kernel,
        after,
        [me, scales, latent, *[array for entry in parts for array in entry[0].arrays]],
        grid=(micro, turns),
        in_specs=[SMEM, whole((16, width)), by_crop((tokens, width))] + [ANY] * sum(counts),
        out_specs=[
            by_crop((tokens, width)),
            by_crop((tokens, width)),
            by_crop((tokens, 3 * width)),
            pl.BlockSpec((1, 2, tokens, tokens), lambda m, h: (m, h, 0, 0)),
            by_crop((tokens, width)),
        ],
        out_shape=[
            shaped((total, width), jnp.float32),
            shaped((total, width), jnp.bfloat16),
            shaped((total, 3 * width), jnp.bfloat16),
            shaped((micro, HEADS, tokens, tokens), jnp.float32),
            shaped((total, width), jnp.bfloat16),
        ],
        scratch_shapes=[
            VMEM((3, width, width), jnp.bfloat16),
            VMEM((width, width), jnp.bfloat16),
            pltpu.SemaphoreType.DMA((4,)),
        ],
        compiler_params=params(52, 2),
        cost_estimate=cost(30),
        name="self_forward",
    )


def run_losses(me, pooled, head, classes, examples, micro, after=()):
    count, width = pooled.shape[0], pooled.shape[1] - MARKS
    parts = (head[0], head[1])
    counts = [len(entry[0].arrays) for entry in parts]
    span = width // 2

    def kernel(me_ref, pooled_ref, *refs):
        groups = (refs[: counts[0]], refs[counts[0] : counts[0] + counts[1]])
        loss_ref, logits_ref, grad_ref, left_s, right_s, sems = refs[counts[0] + counts[1] :]
        me_now = me_ref[0]
        halves = (left_s, right_s)
        for number in range(2):
            parts[number][0].start(
                groups[number], me_now, halves[number], sems.at[number], parts[number][1]
            )
        rows = lax.broadcasted_iota(jnp.int32, (count, 1), 0)
        turn = rows % micro
        marks = pooled_ref[:, width:].astype(jnp.float32)
        labels = (marks[:, 0:1] * 256.0 + marks[:, 1:2]).astype(jnp.int32)
        partner = (marks[:, 2:3] * 256.0 + marks[:, 3:4]).astype(jnp.int32)
        active = marks[:, 4:5]
        pooled_low = pooled_ref[:, :width]
        pooled_wide = pooled_low.astype(jnp.float32)
        columns = lax.broadcasted_iota(jnp.int32, (count, count), 1)
        aimed = lowered((columns == partner * micro + turn).astype(jnp.float32))
        distance = pooled_wide - dot_nn(aimed, pooled_low)
        divisor = jnp.zeros((count, 1), jnp.float32)
        for number in range(micro):
            here = (turn == number).astype(jnp.float32)
            counted = jnp.sum(here * active, axis=0, keepdims=True)
            loss_ref[1 + number : 2 + number] = jnp.broadcast_to(counted, (1, 128))
            counted = jnp.maximum(counted, 1.0)
            divisor = divisor + here * (counted * width**0.5)
        agreement = active * jnp.sum(distance * distance, axis=-1, keepdims=True) / divisor
        pull = (2.0 / micro) * (active / divisor) * distance
        for number in range(2):
            arrived(halves[number], sems.at[number])
        logits = jnp.concatenate([dot_nn(pooled_low, half[...]) for half in halves], axis=1)
        column = lax.broadcasted_iota(jnp.int32, (count, 2 * span), 1)
        logits = jnp.where(column < classes, logits, -1e30)
        top = jnp.max(logits, axis=-1, keepdims=True)
        raised = jnp.exp(logits - top)
        mass = jnp.sum(raised, axis=-1, keepdims=True)
        hot = (column == labels).astype(jnp.float32)
        entropy = top + jnp.log(mass) - jnp.sum(logits * hot, axis=-1, keepdims=True)
        loss = jnp.sum(entropy / examples + agreement, axis=0, keepdims=True) / micro
        loss_ref[0:1] = jnp.broadcast_to(loss, (1, 128))
        grad_logits = lowered((raised / mass - hot) / (examples * micro))
        logits_ref[...] = grad_logits
        grad = pull + sum(
            dot_nt(grad_logits[:, number * span : (number + 1) * span], halves[number][...])
            for number in range(2)
        )
        for number in range(micro):
            own = (rows == me_now * micro + number).astype(jnp.float32)
            aiming = ((partner == me_now) & (turn == number)).astype(jnp.float32)
            grad_ref[number] = jnp.sum(own * grad - aiming * pull, axis=0, keepdims=True)

    vmem = pl.BlockSpec(memory_space=pltpu.VMEM)
    return launch(
        kernel,
        after,
        [me, pooled, *[array for entry in parts for array in entry[0].arrays]],
        in_specs=[SMEM, vmem] + [ANY] * sum(counts),
        out_specs=[vmem] * 3,
        out_shape=[
            shaped((8, 128), jnp.float32),
            shaped((count, width), jnp.bfloat16),
            shaped((micro, 1, width), jnp.float32),
        ],
        scratch_shapes=[
            VMEM((width, span), jnp.bfloat16),
            VMEM((width, span), jnp.bfloat16),
            pltpu.SemaphoreType.DMA((2,)),
        ],
        compiler_params=pltpu.CompilerParams(vmem_limit_bytes=24 * MIB),
        cost_estimate=cost(5),
        name="losses",
    )


class Sender:
    def __init__(self, total, core_rows):
        self.total = total
        self.core_rows = core_rows
        self.groups = total // (2 * core_rows)

    def shapes(self, columns):
        return [shaped((self.groups, self.core_rows, columns), jnp.bfloat16)] * 2

    def start(self, source, core, keep, send, column, sem):
        width = source.shape[1]
        rows = self.core_rows
        for group in range(self.groups):
            for target, side in ((send, 1 - core), (keep, core)):
                spot = pl.multiple_of((2 * group + side) * rows, rows)
                pltpu.make_async_copy(
                    source.at[pl.ds(spot, rows), :],
                    target.at[group, :, column : column + width],
                    sem,
                ).start()


def run_feed_backward(
    me, scales, latent, upstream, steep, first, second, column, micro, pool, after=()
):
    total, width = latent.shape
    tokens = total // micro
    parts = (first, second)
    counts = [len(entry[0].arrays) for entry in parts]
    span = width // 2

    def kernel(me_ref, scale_ref, latent_ref, up_ref, *refs):
        if pool:
            pooled_ref, refs = refs[0], refs[1:]
        steep_ref, refs = refs[0], refs[1:]
        first_refs, refs = refs[: counts[0]], refs[counts[0] :]
        second_refs, refs = refs[: counts[1]], refs[counts[1] :]
        out_ref, gain_ref, low_ref, before_ref, after_ref, first_s, second_s, sems = refs
        step = pl.program_id(0)

        @pl.when(step == 0)
        def _():
            second[0].start(second_refs, me_ref[0], second_s, sems.at[1], second[1])
            first[0].start(first_refs, me_ref[0], first_s, sems.at[0], first[1])
            gain_ref[...] = jnp.zeros(gain_ref.shape, jnp.float32)

        if pool:
            spread = jnp.broadcast_to(pooled_ref[0] / tokens, (tokens, width))
            upstream, gain, bias = norm_back(up_ref[...], scale_ref, 8, spread)
            gain_ref[2:3] += gain
            gain_ref[3:4] += bias
            out_ref[...] = upstream
        else:
            out_ref[...] = up_ref[...]
        low_ref[...] = lowered(out_ref[...])

        @pl.when(step == 0)
        def _():
            arrived(second_s, sems.at[1])

        for number in range(2):
            cut = slice(number * span, (number + 1) * span)
            grad = dot_nt(low_ref[...], second_s[cut, :])
            before_ref[:, cut] = lowered(grad * steep_ref[:, cut].astype(jnp.float32))

        @pl.when(step == 0)
        def _():
            arrived(first_s, sems.at[0])

        back, gain, bias = norm_back(
            latent_ref[...], scale_ref, column, dot_nt(before_ref[...], first_s[...])
        )
        gain_ref[0:1] += gain
        gain_ref[1:2] += bias
        out_ref[...] += back
        after_ref[...] = lowered(out_ref[...])

    in_specs = [SMEM, whole((16, width)), by_crop((tokens, width)), by_crop((tokens, width))]
    operands = [me, scales, latent]
    if pool:
        in_specs.append(by_crop((1, 1, width)))
        operands += list(upstream)
    else:
        operands.append(upstream)
    in_specs += [by_crop((tokens, width))] + [ANY] * sum(counts)
    operands += [steep] + [array for entry in parts for array in entry[0].arrays]
    return launch(
        kernel,
        after,
        operands,
        in_specs,
        grid=(micro,),
        out_specs=[by_crop((tokens, width)), whole((8, width))] + [by_crop((tokens, width))] * 3,
        out_shape=[shaped((total, width), jnp.float32), shaped((8, width), jnp.float32)]
        + [shaped((total, width), jnp.bfloat16)] * 3,
        scratch_shapes=[
            VMEM((width, width), jnp.bfloat16),
            VMEM((width, width), jnp.bfloat16),
            pltpu.SemaphoreType.DMA((2,)),
        ],
        compiler_params=params(48),
        cost_estimate=cost(16),
        name="feed_backward",
    )


def run_self_backward(crop, me, scales, latent, upstream, stored, query, key, value, out, micro, onward, after=()):
    total, width = latent.shape
    tokens = total // micro
    part = width // HEADS
    pair = 2 * part
    turns = HEADS // 2
    packed, attend = stored
    parts = (query, key, value, out)
    counts = [len(entry[0].arrays) for entry in parts]

    def kernel(me_ref, scale_ref, latent_ref, up_ref, packed_ref, attend_ref, *refs):
        groups = []
        at = 0
        for count in counts:
            groups.append(refs[at : at + count])
            at += count
        if onward is not None:
            at += 1
        grad_ref, out_ref, gain_ref, packed_s, out_s, blend_s, sems = refs[at:]
        turn = pl.program_id(0)

        @pl.when(turn == 0)
        def _():
            out[0].start(groups[3], me_ref[0], out_s, sems.at[3], out[1])
            for number in range(3):
                parts[number][0].start(
                    groups[number], me_ref[0], packed_s.at[number], sems.at[number], parts[number][1]
                )
            arrived(out_s, sems.at[3])
            blend_s[...] = lowered(dot_nt(lowered(up_ref[...]), out_s[...]))

        base = pl.multiple_of(turn * pair, pair)
        queries = packed_ref[:, pl.ds(base, pair)]
        keys = packed_ref[:, pl.ds(pl.multiple_of(width + base, pair), pair)]
        values = packed_ref[:, pl.ds(pl.multiple_of(2 * width + base, pair), pair)]
        blends = blend_s[:, pl.ds(base, pair)]
        grads = ([], [], [])
        for head in range(2):
            cut = slice(head * part, (head + 1) * part)
            attend = attend_ref[0, head]
            grad_attend = dot_nt(blends[:, cut], values[:, cut])
            scores = lowered(softmax_back(attend, grad_attend) * part ** (-0.5))
            grads[2].append(lowered(dot_tn(lowered(attend), blends[:, cut])))
            grads[0].append(lowered(dot_nn(scores, keys[:, cut])))
            grads[1].append(lowered(dot_tn(scores, queries[:, cut])))
        for number in range(3):
            spot = pl.ds(pl.multiple_of(number * width + base, pair), pair)
            grad_ref[:, spot] = jnp.concatenate(grads[number], axis=1)

        @pl.when(turn == turns - 1)
        def _():
            for number in range(3):
                arrived(packed_s.at[number], sems.at[number])
            grad_hidden = sum(
                dot_nt(grad_ref[:, number * width : (number + 1) * width], packed_s[number])
                for number in range(3)
            )
            back, gain, bias = norm_back(latent_ref[...], scale_ref, 4, grad_hidden)
            gain_ref[0:1] = gain
            gain_ref[1:2] = bias
            out_ref[...] = up_ref[...] + back

    def crop_rows(columns):
        return pl.BlockSpec((tokens, columns), lambda h: (crop, 0))

    operands = [me, scales, latent, upstream, packed, attend]
    operands += [array for entry in parts for array in entry[0].arrays]
    aliases = {}
    if onward is not None:
        aliases = {len(operands): 1}
        operands.append(onward)
    return launch(
        kernel,
        after,
        operands,
        grid=(turns,),
        in_specs=[
            SMEM,
            whole((16, width)),
            crop_rows(width),
            crop_rows(width),
            crop_rows(3 * width),
            pl.BlockSpec((1, 2, tokens, tokens), lambda h: (crop, h, 0, 0)),
        ]
        + [ANY] * (sum(counts) + len(aliases)),
        input_output_aliases=aliases,
        out_specs=[whole((tokens, 3 * width)), crop_rows(width), whole((8, width))],
        out_shape=[
            shaped((tokens, 3 * width), jnp.bfloat16),
            shaped((total, width), jnp.float32),
            shaped((8, width), jnp.float32),
        ],
        scratch_shapes=[
            VMEM((3, width, width), jnp.bfloat16),
            VMEM((width, width), jnp.bfloat16),
            VMEM((tokens, width), jnp.bfloat16),
            pltpu.SemaphoreType.DMA((4,)),
        ],
        compiler_params=params(56),
        cost_estimate=cost(20),
        name="self_backward",
    )


def run_weights(me, products, sender, columns, after=()):
    flat = []
    for lefts, rights, _ in products:
        for array, _, _ in lefts + rights:
            if not any(array is known for known in flat):
                flat.append(array)
    where = {id(array): number for number, array in enumerate(flat)}
    count = len(columns)
    depth = products[0][0][0][0].shape[1]
    width = max(last for _, _, places in products for _, last, _, _ in places)

    def kernel(me_ref, *refs):
        sources, refs = refs[: len(flat)], refs[len(flat) :]
        targets, (mat_s, sem) = refs[: 2 * count], refs[2 * count :]
        core = (me_ref[0] // me_ref[1]) % 2
        for number, (lefts, rights, places) in enumerate(products):
            for column, last, buffer, spot in places:
                mat_s[number, :, column:last] = lowered(
                    sum(
                        dot_tn(
                            sources[where[id(left)]][begin : begin + size, :],
                            sources[where[id(right)]][:, at + column : at + last],
                        )
                        for (left, begin, size), (right, at, _) in zip(lefts, rights)
                    )
                )
                sender.start(
                    mat_s.at[number, :, column:last],
                    core,
                    targets[2 * buffer],
                    targets[2 * buffer + 1],
                    spot,
                    sem,
                )
        for number, (lefts, rights, places) in enumerate(products):
            for column, last, buffer, spot in places:
                arrived(mat_s.at[number, :, column:last], sem)

    vmem = pl.BlockSpec(memory_space=pltpu.VMEM)
    return launch(
        kernel,
        after,
        [me] + flat,
        [SMEM] + [vmem] * len(flat),
        out_specs=[ANY] * (2 * count),
        out_shape=[shape for number in columns for shape in sender.shapes(number)],
        scratch_shapes=[
            VMEM((len(products), depth, width), jnp.bfloat16),
            pltpu.SemaphoreType.DMA,
        ],
        compiler_params=pltpu.CompilerParams(vmem_limit_bytes=40 * MIB),
        cost_estimate=cost(3 * len(products)),
        name="weights",
    )


def run_cross_backward(
    me, scales, initial, upstream, stored, gains, first, second, micro, sender, after=()
):
    total, width = upstream.shape
    tokens = total // micro
    queries, attend, pairs = stored
    spots = pairs.shape[1]
    parts = (first, second)
    counts = [len(entry[0].arrays) for entry in parts]
    small_columns = tokens + 128

    def kernel(me_ref, scale_ref, initial_ref, up_ref, query_ref, attend_ref, pair_ref, gains_ref, *refs):
        first_refs, refs = refs[: counts[0]], refs[counts[0] :]
        second_refs, refs = refs[: counts[1]], refs[counts[1] :]
        query_out, pair_out, keep, send, first_s, second_s, up_s, back_s, small_s, sems = refs
        step = pl.program_id(0)
        core = (me_ref[0] // me_ref[1]) % 2

        @pl.when(step == 0)
        def _():
            second[0].start(second_refs, me_ref[0], second_s, sems.at[1], second[1])
            first[0].start(first_refs, me_ref[0], first_s, sems.at[0], first[1])
            up_s[...] = jnp.zeros(up_s.shape, jnp.float32)
            back_s[...] = jnp.zeros(back_s.shape, jnp.float32)
            arrived(second_s, sems.at[1])

        keys, values = pair_ref[0, :, :width], pair_ref[0, :, width:]
        attend = attend_ref[0]
        blend = lowered(dot_nt(lowered(up_ref[...]), second_s[...]))
        scores = lowered(softmax_back(attend, dot_nt(blend, values)) * width ** (-0.5))
        query_out[...] = lowered(dot_nn(scores, keys))
        pair_out[:, :width] = lowered(dot_tn(scores, query_ref[...]))
        pair_out[:, width:] = lowered(dot_tn(lowered(attend), blend))
        up_s[...] += up_ref[...]

        @pl.when(step == 0)
        def _():
            arrived(first_s, sems.at[0])

        back_s[...] += dot_nt(query_out[...], first_s[...])

        @pl.when(step == micro - 1)
        def _():
            back, gain, bias = norm_back(initial_ref[...], scale_ref, 0, back_s[...])
            gains_all = jnp.concatenate(
                [gain, bias, gains_ref[2:, :], jnp.zeros((128 - gains_ref.shape[0], width), jnp.float32)], axis=0
            )
            small_s[:, :tokens] = lowered((up_s[...] + back).T)
            small_s[:, tokens:] = lowered(gains_all.T)
            sender.start(small_s, core, keep, send, 0, sems.at[2])
            arrived(small_s, sems.at[2])

    return launch(
        kernel,
        after,
        [me, scales, initial, upstream, queries, attend, pairs, gains]
        + [array for entry in parts for array in entry[0].arrays],
        [
            SMEM,
            whole((16, width)),
            whole((tokens, width)),
            by_crop((tokens, width)),
            whole((tokens, width)),
            by_crop((1, tokens, spots)),
            by_crop((1, spots, 2 * width)),
            whole((16, width)),
        ]
        + [ANY] * sum(counts),
        grid=(micro,),
        out_specs=[by_crop((tokens, width)), by_crop((spots, 2 * width)), ANY, ANY],
        out_shape=[
            shaped((total, width), jnp.bfloat16),
            shaped((micro * spots, 2 * width), jnp.bfloat16),
        ]
        + sender.shapes(small_columns),
        scratch_shapes=[
            VMEM((width, width), jnp.bfloat16),
            VMEM((width, width), jnp.bfloat16),
            VMEM((tokens, width), jnp.float32),
            VMEM((tokens, width), jnp.float32),
            VMEM((width, small_columns), jnp.bfloat16),
            pltpu.SemaphoreType.DMA((3,)),
        ],
        compiler_params=params(48),
        cost_estimate=cost(16),
        name="cross_backward",
    )


def run_last_weights(me, hidden, grad_queries, grad_pairs, pictures, sender, kv_sender, after=()):
    tokens, width = hidden.shape
    micro = grad_queries.shape[0] // tokens
    channels = pictures.shape[1]

    def kernel(me_ref, hidden_ref, query_ref, pair_ref, pic_ref, keep, send, keep_kv, send_kv, mat_s, kv_s, sems):
        core = (me_ref[0] // me_ref[1]) % 2
        span = width // 2
        for number in range(2):
            cut = slice(number * span, (number + 1) * span)
            mat_s[:, cut] = lowered(
                sum(
                    dot_tn(hidden_ref[...], query_ref[crop * tokens : (crop + 1) * tokens, cut])
                    for crop in range(micro)
                )
            )
        sender.start(mat_s, core, keep, send, 0, sems.at[0])
        kv_s[...] = lowered(dot_tn(pair_ref[...], pic_ref[...]))
        kv_sender.start(kv_s, core, keep_kv, send_kv, 0, sems.at[1])
        arrived(mat_s, sems.at[0])
        arrived(kv_s, sems.at[1])

    vmem = pl.BlockSpec(memory_space=pltpu.VMEM)
    return launch(
        kernel,
        after,
        [me, hidden, grad_queries, grad_pairs, pictures],
        [SMEM] + [vmem] * 4,
        out_specs=[ANY] * 4,
        out_shape=sender.shapes(width) + kv_sender.shapes(channels),
        scratch_shapes=[
            VMEM((width, width), jnp.bfloat16),
            VMEM((2 * width, channels), jnp.bfloat16),
            pltpu.SemaphoreType.DMA((2,)),
        ],
        compiler_params=pltpu.CompilerParams(vmem_limit_bytes=32 * MIB),
        cost_estimate=cost(6),
        name="last_weights",
    )


def run_shards(matrices, kv_weight, norm_gains, head_weight, latent_init, columns):
    rows = matrices.shape[0]
    tokens, gains = latent_init.shape[1], norm_gains.shape[1]
    channels = kv_weight.shape[1]
    wide_channels = -(-channels // 128) * 128
    classes = head_weight.shape[1]
    width = matrices.shape[1] // 10
    small = tokens + 128

    def kernel(mat_ref, kv_ref, gain_ref, head_ref, latent_ref, first_ref, *refs):
        first_ref[...] = jnp.zeros(first_ref.shape, jnp.bfloat16)
        first_ref[:, :tokens] = lowered(latent_ref[...])
        first_ref[:, tokens : tokens + gains] = lowered(gain_ref[...])
        for side in range(2):
            at = small + side * wide_channels
            first_ref[:, at : at + channels] = lowered(kv_ref[side * rows : (side + 1) * rows, :])
        for (begin, end), ref in zip(columns, refs):
            ref[...] = lowered(mat_ref[:, begin * width : end * width])
        refs[-1][...] = jnp.zeros(refs[-1].shape, jnp.bfloat16)
        refs[-1][:, :classes] = lowered(head_ref[...])

    widths = [small + 2 * wide_channels] + [(end - begin) * width for begin, end in columns] + [width]
    vmem = pl.BlockSpec(memory_space=pltpu.VMEM)
    return pl.pallas_call(
        kernel,
        in_specs=[vmem] * 5,
        out_specs=[vmem] * len(widths),
        out_shape=[shaped((rows, number), jnp.bfloat16) for number in widths],
        compiler_params=pltpu.CompilerParams(vmem_limit_bytes=24 * MIB),
        cost_estimate=cost(3),
        name="shards",
    )(matrices, kv_weight, norm_gains, head_weight, latent_init)


def run_join(targets, passing, after):
    moves = [move for _, parts in targets for move in parts]
    count, kept = len(moves), len(passing)

    def kernel(*refs):
        sources = refs[:count]
        outs = refs[count + kept : count + kept + len(targets)]
        sems = refs[-1]
        copies = []
        at = 0
        for target, (_, parts) in zip(outs, targets):
            for _, cut, first in parts:
                source = sources[at] if cut is None else sources[at].at[:, cut]
                size = 1 if len(source.shape) == 2 else source.shape[0]
                spot = target.at[first] if len(source.shape) == 2 else target.at[first : first + size]
                copies.append(pltpu.make_async_copy(source, spot, sems.at[at]))
                at += 1
        for copy in copies:
            copy.start()
        for copy in copies:
            copy.wait()

    outs = launch(
        kernel,
        after,
        [move[0] for move in moves] + list(passing),
        [ANY] * (count + kept),
        out_specs=[ANY] * (len(targets) + kept),
        out_shape=[shaped(shape, jnp.bfloat16) for shape, _ in targets]
        + [shaped(array.shape, array.dtype) for array in passing],
        scratch_shapes=[pltpu.SemaphoreType.DMA((count,))],
        input_output_aliases={count + number: len(targets) + number for number in range(kept)},
        compiler_params=pltpu.CompilerParams(vmem_limit_bytes=1 * MIB),
        cost_estimate=cost(3),
        name="join",
    )
    return outs[: len(targets)], outs[len(targets) :]


def run_fold(me, parts, after):
    depth = 4
    operands = [me]
    in_specs = [SMEM]
    out_specs = []
    out_shape = []
    for terms, axis in parts:
        groups, rows, columns = terms[0].shape
        each = groups // depth
        for term in terms:
            operands.append(term)
            in_specs.append(pl.BlockSpec((each, rows, columns), lambda z: (z, 0, 0)))
        if axis == "x":
            block = (each, rows // 2, columns)
        else:
            block = (1, rows, columns)
        for _ in range(2):
            out_specs.append(pl.BlockSpec(block, lambda z: (z, 0, 0)))
            out_shape.append(shaped((block[0] * depth,) + block[1:], jnp.bfloat16))

    def kernel(me_ref, *refs):
        at = 0
        out = sum(len(terms) for terms, _ in parts)
        mine = {"x": me_ref[0] % 2, "y": (me_ref[0] // 4) % 2}
        for terms, axis in parts:
            sources = refs[at : at + len(terms)]
            at += len(terms)
            for side in range(2):
                spot = mine[axis] if side == 0 else 1 - mine[axis]
                if axis == "x":
                    rows = sources[0].shape[1] // 2
                    cut = (slice(None), pl.ds(pl.multiple_of(spot * rows, rows), rows), slice(None))
                else:
                    cut = (pl.ds(spot, 1), slice(None), slice(None))
                refs[out][...] = lowered(sum(source[cut].astype(jnp.float32) for source in sources))
                out += 1

    outs = launch(
        kernel,
        after,
        operands,
        in_specs,
        grid=(depth,),
        out_specs=out_specs,
        out_shape=out_shape,
        compiler_params=params(32),
        cost_estimate=cost(4),
        name="fold",
    )
    return [(outs[2 * number], outs[2 * number + 1]) for number in range(len(parts))]


def run_fold_z(me, parts, after):
    depth = 4

    def kernel(me_ref, *refs):
        mine = me_ref[0] // 8
        at = 0
        out = sum(len(terms) for terms in parts)
        for terms in parts:
            sources = refs[at : at + len(terms)]
            at += len(terms)
            for k in range(depth):
                spot = mine ^ k
                refs[out][...] = lowered(
                    sum(source[pl.ds(spot, 1)].astype(jnp.float32) for source in sources)
                )[0]
                out += 1

    vmem = pl.BlockSpec(memory_space=pltpu.VMEM)
    operands = [me] + [term for terms in parts for term in terms]
    shapes = [
        shaped(terms[0].shape[1:], jnp.bfloat16) for terms in parts for _ in range(depth)
    ]
    outs = launch(
        kernel,
        after,
        operands,
        [SMEM] + [vmem] * (len(operands) - 1),
        out_specs=[vmem] * len(shapes),
        out_shape=shapes,
        compiler_params=pltpu.CompilerParams(vmem_limit_bytes=24 * MIB),
        cost_estimate=cost(3),
        name="fold_z",
    )
    return [outs[depth * number : depth * (number + 1)] for number in range(len(parts))]


def digits():
    n_wide = lax.axis_size("wide")
    n_narrow = lax.axis_size("narrow")
    rest = n_wide // 2
    top = min(4, rest)
    return (
        ("z", n_narrow * n_wide // top, top),
        ("y", 2 * n_narrow, rest // top),
        ("c", n_narrow, 2),
        ("x", 1, n_narrow),
    )


def device_index():
    return lax.axis_index("wide") * lax.axis_size("narrow") + lax.axis_index("narrow")


def exchange(values, offset):
    total = lax.axis_size(AXES)
    return lax.ppermute(values, AXES, [(i, i ^ offset) for i in range(total)])


class Gather:
    def __init__(self, shard, left, plain):
        self.shard = shard
        self.widths = (left, shard.shape[1] - left)
        self.rows = shard.shape[0]
        self.table = {name: (stride, size) for name, stride, size in digits()}
        self.names = (("y", "x"), ("x", "y"))
        self.plain = plain

    def send_z(self):
        stride, size = self.table["z"]
        self.got = [exchange(self.shard, k * stride) for k in range(1, size)]
        return self.got

    def join(self, targets, passing, after):
        if self.plain:
            flats = []
            for _, parts in targets:
                flats.append(
                    jnp.concatenate(
                        [
                            array if array.ndim == 3 else array[None, :, cut]
                            for array, cut, _ in parts
                        ]
                    )
                )
            return flats, passing
        return run_join(targets, passing, after)

    def join_z(self, passing=(), after=()):
        stride, size = self.table["z"]
        pieces = [self.shard] + self.got
        targets = []
        at = 0
        for width in self.widths:
            parts = [(piece, slice(at, at + width), k) for k, piece in enumerate(pieces)]
            targets.append(((size, self.rows, width), parts))
            at += width
        self.flats, passing = self.join(targets, passing, after)
        self.offsets = [[k * stride for k in range(size)]] * 2
        return passing

    def send(self, turn):
        self.got = []
        for half in range(2):
            stride, size = self.table[self.names[half][turn]]
            self.got.append([exchange(self.flats[half], k * stride) for k in range(1, size)])
        return self.got[0] + self.got[1]

    def pieces(self, turn):
        halves = []
        for half in range(2):
            stride, size = self.table[self.names[half][turn]]
            arrays = [self.flats[half]] + self.got[half]
            halves.append(
                (arrays, [[offset ^ (k * stride) for offset in self.offsets[half]] for k in range(size)])
            )
        return halves

    def join_first(self, passing=(), after=()):
        targets = []
        offsets = []
        for arrays, groups in self.pieces(0):
            count = arrays[0].shape[0]
            parts = [(array, None, k * count) for k, array in enumerate(arrays)]
            targets.append(((count * len(arrays),) + arrays[0].shape[1:], parts))
            offsets.append([offset for group in groups for offset in group])
        self.flats, passing = self.join(targets, passing, after)
        self.offsets = offsets
        return passing

    def send_across(self):
        stride = self.table["c"][0]
        self.state = []
        fresh = []
        for arrays, offsets in self.pieces(1):
            sent = [exchange(array, stride) for array in arrays]
            fresh += sent
            self.state.append(
                (
                    arrays + sent,
                    offsets + [[offset ^ stride for offset in group] for group in offsets],
                )
            )
        return fresh

    def done(self):
        halves = []
        me = device_index()
        total = lax.axis_size(AXES)
        for arrays, offsets in self.state:
            if not self.plain:
                halves.append(Half(arrays, offsets, self.rows))
            else:
                flat = jnp.concatenate(arrays)
                spots = jnp.argsort(jnp.array([o for group in offsets for o in group]) ^ me)
                flat = jnp.take(flat, spots, axis=0).reshape(1, total * self.rows, -1)
                halves.append(Half([flat], None, total * self.rows))
        return halves


class Scatter:
    def __init__(self, me, parts, turns, plain):
        self.me = me
        self.parts = parts
        self.turns = turns
        self.plain = plain
        self.table = {name: (stride, size) for name, stride, size in digits()}

    def send_across(self):
        stride = self.table["c"][0]
        sizes = tuple(self.table[name][1] for name in ("z", "y", "x"))
        fresh = [exchange(send, stride) for _, send in self.parts]
        self.state = []
        for (keep, _), received in zip(self.parts, fresh):
            terms = [keep, received]
            if self.plain:
                rows = keep.shape[0] * keep.shape[1] // (sizes[0] * sizes[1] * sizes[2])
                terms = [term.reshape(sizes + (rows, keep.shape[2])) for term in terms]
            self.state.append((["z", "y", "x"], terms))
        return fresh

    def send(self, turn, after=()):
        fresh = []
        if not self.plain:
            names = [ways[turn] for ways in self.turns]
            if turn < 2:
                pairs = run_fold(
                    self.me, [(terms, name) for (_, terms), name in zip(self.state, names)], after
                )
            else:
                pairs = run_fold_z(self.me, [terms for _, terms in self.state], after)
            self.state = []
            for (kept, *sends), name in zip(pairs, names):
                stride = self.table[name][0]
                sent = [exchange(send, (k + 1) * stride) for k, send in enumerate(sends)]
                fresh += sent
                self.state.append((None, [kept] + sent))
            return fresh
        me = device_index()
        for number, (left, terms) in enumerate(self.state):
            name = self.turns[number][turn]
            stride, size = self.table[name]
            mine = (me // stride) % size
            axis = left.index(name)

            def part(index):
                return lowered(
                    sum(
                        lax.dynamic_index_in_dim(term, index, axis, keepdims=False).astype(jnp.float32)
                        for term in terms
                    )
                )

            sent = [exchange(part(mine ^ k), k * stride) for k in range(1, size)]
            fresh += sent
            self.state[number] = ([entry for entry in left if entry != name], [part(mine)] + sent)
        return fresh

    def done(self):
        return [sum(term.astype(jnp.float32) for term in terms) for _, terms in self.state]


def share(values):
    total = lax.axis_size(AXES)
    spread = jnp.broadcast_to(values[None], (total,) + values.shape)
    return lax.all_to_all(spread, AXES, 0, 0, tiled=True)


def on_device(
    pixels,
    labels,
    partner,
    pair_on,
    step_count,
    matrices,
    kv_weight,
    norm_gains,
    head_weight,
    latent_init,
    matrices_first,
    kv_first,
    gains_first,
    head_first,
    latent_first,
    matrices_second,
    kv_second,
    gains_second,
    head_second,
    latent_second,
):
    axis_count = lax.axis_size(AXES)
    n_narrow = lax.axis_size("narrow")
    index = device_index()
    me = jnp.stack([index, jnp.int32(n_narrow)]).astype(jnp.int32)
    micro = pixels.shape[0]
    tokens = latent_init.shape[1]
    width = matrices.shape[1] // 10
    rows = matrices.shape[0]
    channels = pixels.shape[3]
    wide_channels = -(-channels // 128) * 128
    classes = head_weight.shape[1]

    half = width // 2
    small_columns = tokens + 128
    plain = rows % 16 != 0 or tuple(size for _, _, size in digits()) != (4, 2, 2, 2)
    pictures = jnp.pad(pixels[:, 0], ((0, 0), (0, 0), (0, wide_channels - channels)))
    blocks = ((0, 2), (2, 4), (4, 8), (8, 10))
    shards = run_shards(matrices, kv_weight, norm_gains, head_weight, latent_init, blocks)
    lefts = [small_columns] + [(end - begin) * half for begin, end in blocks] + [half]
    chunks = [Gather(shard, left, plain) for shard, left in zip(shards, lefts)]

    a, b, c, d, e, f = chunks
    a.send_z()
    b.send_z()
    (c.shard,) = a.join_z([c.shard])
    a.send(0)
    c.send_z()
    (d.shard,) = b.join_z([d.shard], after=a.flats)
    b.send(0)
    a.join_first(after=b.flats)
    a.send(1)
    d.send_z()
    (e.shard,) = c.join_z([e.shard], after=a.flats)
    c.send(0)
    b.join_first(after=c.flats)
    b.send(1)
    a.send_across()
    e.send_z()
    (f.shard,) = d.join_z([f.shard], after=b.flats)
    d.send(0)
    c.join_first(after=d.flats)
    c.send(1)
    b.send_across()
    weights = {}
    small_half, kv_half = a.done()
    weights[0], weights[1] = [(entry, 0) for entry in b.done()]
    kv_column = 0
    if kv_half.offsets is None:
        array = kv_half.arrays[0].reshape(axis_count, rows, 2, wide_channels)
        array = array.transpose(0, 2, 1, 3).reshape(1, 2 * width, wide_channels)
        kv_half = Half([array], None, 2 * width)
    latent_one, blended, attend, pairs, initial, hidden_zero, queries, scales = run_cross_forward(
        me, pictures, (small_half, 0), (kv_half, 0), weights[0], weights[1], width, tokens,
        after=c.flats,
    )
    f.send_z()
    e.join_z(after=[latent_one])
    e.send(0)
    d.join_first(after=e.flats)
    d.send(1)
    c.send_across()
    weights[2], weights[3] = [(entry, 0) for entry in c.done()]
    latent_two, hidden_one, active_one, steep_one = run_feed_forward(
        me, scales, latent_one, weights[2], weights[3], 2, micro, False,
        after=d.flats,
    )
    f.join_z(after=[latent_two])
    f.send(0)
    e.join_first(after=f.flats)
    e.send(1)
    d.send_across()
    left, right = d.done()
    for number in range(2):
        weights[4 + number] = (left, number * width)
        weights[6 + number] = (right, number * width)
    latent_three, hidden_two, packed, attend_self, blended_self = run_self_forward(
        me, scales, latent_two, weights[4], weights[5], weights[6], weights[7], micro,
        after=e.flats,
    )
    f.join_first(after=[latent_three])
    f.send(1)
    e.send_across()
    weights[8], weights[9] = [(entry, 0) for entry in e.done()]
    result, hidden_three, active_three, steep_three, pooled = run_feed_forward(
        me, scales, latent_three, weights[8], weights[9], 6, micro, True,
        after=f.flats,
    )
    f.send_across()
    marks = jnp.stack(
        [labels[:, 0] // 256, labels[:, 0] % 256, partner[:, 0] // 256, partner[:, 0] % 256, pair_on[:, 0]],
        axis=1,
    )
    marks = jnp.pad(lowered(marks), ((0, 0), (0, MARKS - marks.shape[1])))
    pooled_all = share(jnp.concatenate([pooled.reshape(micro, width), marks], axis=1))
    pooled_all = pooled_all.reshape(axis_count * micro, width + MARKS)
    loss_tile, grad_logits, grad_pooled = run_losses(
        me, pooled_all, [(entry, 0) for entry in f.done()], classes, axis_count, micro
    )
    total_loss = loss_tile[0, 0]
    counts = loss_tile[1 : 1 + micro, 0].astype(jnp.int32)
    pooled_rows = lax.dynamic_slice_in_dim(pooled_all, index * rows, rows, axis=1)
    grad_head = dot_tn(pooled_rows, grad_logits)[:, :classes]

    sender = Sender(width, n_narrow * rows)
    kv_sender = Sender(2 * width, 2 * n_narrow * rows)
    turns = (("x", "y", "z"), ("y", "x", "z"))
    wide_half = width + half
    columns = (wide_half, wide_half)
    total_tokens = micro * tokens

    def triple(pairs_of):
        places = (
            [(0, half, 0, 0), (half, width, 0, half)],
            [(0, half, 1, 0), (half, width, 1, half)],
            [(0, half, 0, width), (half, width, 1, width)],
        )
        return [(lefts, rights, place) for (lefts, rights), place in zip(pairs_of, places)]

    def single(left, right):
        return [(left, 0, total_tokens)], [(right, 0, 0)]

    upstream, gain_high, low, before, behind = run_feed_backward(
        me, scales, latent_three, (result, grad_pooled), steep_three, weights[8], weights[9], 6, micro, True
    )
    parts = run_weights(
        me,
        triple((single(active_three, low), single(hidden_three, before), single(blended_self, behind))),
        sender,
        columns,
    )
    one = Scatter(me, [parts[0:2], parts[2:4]], turns, plain)
    one_c = one.send_across()
    grads = []
    gain_mid = 0.0
    onward = None
    for crop in range(micro):
        waits = ()
        if crop == 1:
            one_x = one.send(0, after=[onward])
            waits = [one.state[0][1][0]]
        grad_packed, onward, gain = run_self_backward(
            crop, me, scales, latent_two, upstream, (packed, attend_self),
            weights[4], weights[5], weights[6], weights[7], micro, onward, after=waits,
        )
        grads.append(grad_packed)
        gain_mid = gain_mid + gain
    upstream = onward
    one_y = one.send(1, after=[onward])
    parts = run_weights(
        me,
        triple(
            [
                (
                    [(hidden_two, crop * tokens, tokens) for crop in range(micro)],
                    [(grads[crop], number * width, 0) for crop in range(micro)],
                )
                for number in range(3)
            ]
        ),
        sender,
        columns,
        after=[one.state[0][1][0]],
    )
    two = Scatter(me, [parts[0:2], parts[2:4]], turns, plain)
    two_c = two.send_across()
    one_z = one.send(2, after=[parts[0]])
    upstream, gain_low, low, before, behind = run_feed_backward(
        me, scales, latent_one, upstream, steep_one, weights[2], weights[3], 2, micro, False,
        after=[one.state[0][1][0]],
    )
    two_x = two.send(0, after=[low])
    parts = run_weights(
        me,
        triple((single(active_one, low), single(hidden_one, before), single(blended, behind))),
        sender,
        columns,
        after=[two.state[0][1][0]],
    )
    three = Scatter(me, [parts[0:2], parts[2:4]], turns, plain)
    three_c = three.send_across()
    two_y = two.send(1, after=[parts[0]])
    gains = jnp.concatenate(
        [
            jnp.zeros((2, width), jnp.float32),
            gain_low[:2],
            gain_mid[:2],
            gain_high[:4],
            jnp.zeros((6, width), jnp.float32),
        ]
    )
    grad_queries, grad_pairs, *small_parts = run_cross_backward(
        me, scales, initial, upstream, (queries, attend, pairs), gains,
        weights[0], weights[1], micro, sender, after=[two.state[0][1][0]],
    )
    three_x = three.send(0, after=[grad_queries])
    two_z = two.send(2, after=[three.state[0][1][0]])
    parts = run_last_weights(
        me, hidden_zero, grad_queries, grad_pairs, pictures.reshape(-1, wide_channels), sender, kv_sender,
        after=[two.state[0][1][0]],
    )
    four = Scatter(
        me, [parts[0:2], small_parts, parts[2:4]], (turns[0], turns[1], turns[1]), plain
    )
    four.send_across()
    three.send(1, after=[parts[0]])
    four.send(0, after=[three.state[0][1][0]])
    three.send(2, after=[four.state[0][1][0]])
    four.send(1, after=[three.state[0][1][0]])
    four.send(2)
    nine, eight = one.done()
    four_, five = two.done()
    three_, two_ = three.done()
    zero, rest, grad_kv = four.done()
    grad_matrices = jnp.concatenate(
        [
            zero,
            three_[:, width:],
            two_[:, width:],
            two_[:, :width],
            three_[:, :width],
            four_[:, :width],
            five[:, :width],
            four_[:, width:],
            five[:, width:],
            nine[:, width:],
            eight[:, width:],
            eight[:, :width],
            nine[:, :width],
        ],
        axis=1,
    )
    shares = (
        grad_matrices,
        grad_kv[:, :channels],
        rest[:, tokens : tokens + 10],
        grad_head,
        rest[:, :tokens],
    )
    square = jnp.zeros((), jnp.float32)
    for member in shares:
        square = square + jnp.sum(member * member)
    square = jnp.sum(share(jnp.broadcast_to(square, (128,))), axis=0)[0]
    grad_norm = jnp.sqrt(square)
    factor = jnp.minimum(1.0, THRESH / grad_norm)
    correction = 1.0 - jnp.power(0.5, step_count[0].astype(jnp.float32))
    masters = (matrices, kv_weight, norm_gains, head_weight, latent_init)
    firsts = (matrices_first, kv_first, gains_first, head_first, latent_first)
    seconds = (matrices_second, kv_second, gains_second, head_second, latent_second)
    results = []
    for index, (grad_item, master, moment_one, moment_two) in enumerate(
        zip(shares, masters, firsts, seconds)
    ):
        clipped = grad_item * factor
        moment_one = 0.5 * moment_one + 0.5 * clipped
        moment_two = 0.5 * moment_two + 0.5 * clipped * clipped
        if index == 2 or index == 4:
            results = results + [moment_one, moment_two, clipped]
        else:
            master = master - RATE * (
                moment_one / correction / (jnp.sqrt(moment_two / correction) + TINY)
                + DECAY * master
            )
            results = results + [moment_one, moment_two, master]
    return (
        total_loss,
        grad_norm,
        counts,
        results[0],
        results[1],
        results[2],
        results[3],
        results[4],
        results[5],
        results[6],
        results[7],
        results[8],
        results[9],
        results[10],
        results[11],
        results[12],
        results[13],
        results[14],
    )


def solution(mesh):
    in_specs = (
        P(None, ("wide", "narrow"), None, None),
        P(None, ("wide", "narrow")),
        P(None, ("wide", "narrow")),
        P(None, ("wide", "narrow")),
        P(),
        P(("wide", "narrow"), None),
        P(("wide", "narrow"), None),
        P(("wide", "narrow"), None),
        P(("wide", "narrow"), None),
        P(("wide", "narrow"), None),
        P(("wide", "narrow"), None),
        P(("wide", "narrow"), None),
        P(("wide", "narrow"), None),
        P(("wide", "narrow"), None),
        P(("wide", "narrow"), None),
        P(("wide", "narrow"), None),
        P(("wide", "narrow"), None),
        P(("wide", "narrow"), None),
        P(("wide", "narrow"), None),
        P(("wide", "narrow"), None),
    )
    out_specs = (
        P(),
        P(),
        P(),
        P(("wide", "narrow"), None),
        P(("wide", "narrow"), None),
        P(("wide", "narrow"), None),
        P(("wide", "narrow"), None),
        P(("wide", "narrow"), None),
        P(("wide", "narrow"), None),
        P(("wide", "narrow"), None),
        P(("wide", "narrow"), None),
        P(("wide", "narrow"), None),
        P(("wide", "narrow"), None),
        P(("wide", "narrow"), None),
        P(("wide", "narrow"), None),
        P(("wide", "narrow"), None),
        P(("wide", "narrow"), None),
        P(("wide", "narrow"), None),
    )
    return jax.shard_map(
        on_device, mesh=mesh, in_specs=in_specs, out_specs=out_specs, check_vma=False
    )
```

time: 914 us -> 623 us (0.68)
  Pallas kernels: 0 us -> 257 us
  matrix products: 222 us -> 1.57 us
  other arithmetic: 135 us -> 15.3 us
  waiting for transfers between devices: 229 us -> 128 us
  local copies, waits for them, and re-layouts: 124 us -> 64.6 us
  starting transfers between devices: 181 us -> 139 us
    pallas_call x0 -> x39, Pallas kernels: none -> 257 us  [the longest x38 257 us: launch(): pl.pallas_call(inner, in_specs=list(in_specs) + [ANY] * extra, **rest)]
    dot_general x41 -> x1, matrix products: 222 us -> 1.57 us  [dot_tn(): lax.dot_general(first_op, second_op, (((0,), (0,)), ((), ())), preferred_...]
    ppermute x156 -> x120, waiting for transfers between devices: 229 us -> 118 us  [exchange(): return lax.ppermute(values, AXES, [(i, i ^ offset) for i in range(total)])]
    ppermute x156 -> x120, starting transfers between devices: 181 us -> 122 us  [exchange(): return lax.ppermute(values, AXES, [(i, i ^ offset) for i in range(total)])]
    select_n x91 -> x0, other arithmetic: 42.7 us -> none  [the longest x88 42.7 us: in_place(): stacked = jnp.where(mine & bit != 0, swapped, stacked)]
    convert_element_type x7 -> x0, local copies, waits for them, and re-layouts: 29.3 us -> none  [the longest x6 28.6 us: lowered(): return values.astype(jnp.bfloat16)]
    reduce_sum x21 -> x1, other arithmetic: 23.4 us -> 0.02 us  [on_device(): square = jnp.sum(share(jnp.broadcast_to(square, (128,))), axis=0)[0]]
    convert_element_type x38 -> x1, other arithmetic: 22.4 us -> 1.32 us  [on_device(): counts = loss_tile[1:1 + micro, 0].astype(jnp.int32)]
  transfers between devices with their start and end apart: 156 -> 122, of which waited for: 61 -> 30; matrix products, arithmetic and copies ran while one was open for 27% -> 3% of each run, Pallas kernels for 0% -> 36%
where the time goes in v2:
time: 623 us; the launch traced here: 614 us
  Pallas kernels  257 us (41%)
  starting transfers between devices  139 us (22%)
  waiting for transfers between devices  128 us (21%)
  local copies, waits for them, and re-layouts  64.6 us (10%)
  other arithmetic  15.3 us (2%)
  between operations  8.09 us (1%)
    pallas_call x38, Pallas kernels, launch(): pl.pallas_call(inner, in_specs=list(in_specs) + [ANY] * extra, **rest)  257 us
    ppermute x120, starting transfers between devices, exchange(): return lax.ppermute(values, AXES, [(i, i ^ offset) for i in range(total)])  122 us
    ppermute x120, waiting for transfers between devices, exchange(): return lax.ppermute(values, AXES, [(i, i ^ offset) for i in range(total)])  118 us
    unnamed x325, local copies, waits for them, and re-layouts  55.9 us
    all_to_all x2, starting transfers between devices, share(): return lax.all_to_all(spread, AXES, 0, 0, tiled=True)  16.6 us
  transfers between devices with their start and end apart: 122, of which 30 were waited for; matrix products, arithmetic and copies ran while one was open for 3% of the time, Pallas kernels for 36%

profile of v2, /device:TPU:0, one launch (start us, length us, event | category | flops | bytes accessed | tf_op | source)
XLA Modules:
  0.0 613.6 jit_solution(14892422947684518862)
XLA Ops:
  15.6 7.0 %collective-permute-start.5 = (bf16[32,2048]{1,0:T(8,128)(2,1)S(1)}, bf16[32,2048]{1,0:T(8,128)(2,1)S(1)}, u32[]{:S(2)}, u32[]{:S(2)}) collective-permute-start(bf16[32,2048]{1,0:T(8,128)(2,1)S(1)} %get-tuple-element.189.refs_0_.refs_4_), channel_id=1, source_target_pairs={{0,8},{1,9},{2,10},{3,11},{4,12},{5,13},{6,14},{7,15},{8,0},{9,1},... | collective-permute-start | bytes 393224 | tf_op jit(solution)/shard_map/ppermute | solution.py:1044
  58.2 17.4 %collective-permute-done.28.refs_2_.refs_6_ = bf16[32,4096]{1,0:T(8,128)(2,1)S(1)} collective-permute-done((bf16[32,4096]{1,0:T(8,128)(2,1)S(1)}, bf16[32,4096]{1,0:T(8,128)(2,1)S(1)}, u32[]{:S(2)}, u32[]{:S(2)}) %collective-permute-start.28) | collective-permute-done | bytes 262176 | tf_op jit(solution)/shard_map/ppermute | solution.py:1044
  95.0 10.8 %collective-permute-done.11.refs_7_ = bf16[8,32,768]{2,1,0:T(8,128)(2,1)} collective-permute-done((bf16[8,32,768]{2,1,0:T(8,128)(2,1)S(1)}, bf16[8,32,768]{2,1,0:T(8,128)(2,1)}, u32[]{:S(2)}, u32[]{:S(2)}) %collective-permute-start.11) | collective-permute-done | bytes 393248 | tf_op jit(solution)/shard_map/ppermute | solution.py:1044
  117.8 18.0 %cross_forward.1 = (f32[1024,1024]{1,0:T(8,128)}, bf16[1024,1024]{1,0:T(8,128)(2,1)}, f32[2,512,272]{2,1,0:T(8,128)}, bf16[2,272,2048]{2,1,0:T(8,128)(2,1)}, f32...) custom-call(s32[2]{0:T(128)S(1)} %pad_add_fusion.refs_0_, ...), custom_call_target="tpu_custom_call" | custom-call | flops 19800000512 | bytes 1048576 | tf_op jit(solution)/shard_map/cross_forward/pallas_call | solution.py:127
  151.1 17.2 %feed_forward.2 = (f32[1024,1024]{1,0:T(8,128)}, bf16[1024,1024]{1,0:T(8,128)(2,1)}, bf16[1024,1024]{1,0:T(8,128)(2,1)}, bf16[1024,1024]{1,0:T(8,128)(2,1)}) custom-call(s32[2]{0:T(128)S(1)} %pad_add_fusion.refs_0_, f32[16,1024]{1,0:T(8,128)S(1)} %get-tuple-element.207.refs_1_, f32[1024,1024]{1,0:T(8,128)} %get-tuple-element.208.refs_8_.refs_2_, ...), custom_call_target="tpu_custom_call" | custom-call | flops 17600000000 | bytes 1048576 | tf_op jit(solution)/shard_map/feed_forward/pallas_call | solution.py:127
  173.7 8.3 %collective-permute-done.47.refs_1_ = bf16[4,32,1024]{2,1,0:T(8,128)(2,1)S(1)} collective-permute-done((bf16[4,32,1024]{2,1,0:T(8,128)(2,1)S(1)}, bf16[4,32,1024]{2,1,0:T(8,128)(2,1)S(1)}, u32[]{:S(2)}, u32[]{:S(2)}) %collective-permute-start.47) | collective-permute-done | bytes 262176 | tf_op jit(solution)/shard_map/ppermute | solution.py:1044
  184.6 8.2 %collective-permute-done.52.refs_4_.refs_7_ = bf16[8,32,1024]{2,1,0:T(8,128)(2,1)S(1)} collective-permute-done((bf16[8,32,1024]{2,1,0:T(8,128)(2,1)S(1)}, bf16[8,32,1024]{2,1,0:T(8,128)(2,1)S(1)}, u32[]{:S(2)}, u32[]{:S(2)}) %collective-permute-start.52) | collective-permute-done | bytes 524320 | tf_op jit(solution)/shard_map/ppermute | solution.py:1044
  194.2 8.2 %collective-permute-done.55.refs_8_.refs_11_ = bf16[8,32,1024]{2,1,0:T(8,128)(2,1)S(1)} collective-permute-done((bf16[8,32,1024]{2,1,0:T(8,128)(2,1)S(1)}, bf16[8,32,1024]{2,1,0:T(8,128)(2,1)S(1)}, u32[]{:S(2)}, u32[]{:S(2)}) %collective-permute-start.55) | collective-permute-done | bytes 524320 | tf_op jit(solution)/shard_map/ppermute | solution.py:1044
  204.0 29.4 %self_forward.1 = (f32[1024,1024]{1,0:T(8,128)}, bf16[1024,1024]{1,0:T(8,128)(2,1)}, bf16[1024,3072]{1,0:T(8,128)(2,1)}, f32[2,8,512,512]{3,2,1,0:T(8,128)}, bf16[1024,1024]{1,0:T(8,128)(2,1)}) custom-call(s32[2]{0:T(128)S(1)} %pad_add_fusion.refs_0_, f32[16,1024]{1,0:T(8,128)S(1)} %copy-done.130, f32[1024,1024]{1,0:T(8,128)} %get-tuple-element.214.refs_8_.refs_2_, ...), custom_call_target="tpu_custom_call" | custom-call | flops 32999999488 | bytes 1048576 | tf_op jit(solution)/shard_map/self_forward/pallas_call | solution.py:127
  238.9 18.9 %feed_forward.3 = (f32[1024,1024]{1,0:T(8,128)}, bf16[1024,1024]{1,0:T(8,128)(2,1)}, bf16[1024,1024]{1,0:T(8,128)(2,1)}, bf16[1024,1024]{1,0:T(8,128)(2,1)}, bf16[2,1,1024]{2,1,0:T(2,128)(2,1)S(1)}) custom-call(s32[2]{0:T(128)S(1)} %copy-done.86, f32[16,1024]{1,0:T(8,128)S(1)} %copy-done.131, f32[1024,1024]{1,0:T(8,128)} %get-tuple-element.220.refs_4_.refs_2_, ...), custom_call_target="tpu_custom_call" | custom-call | flops 17600000000 | bytes 1048576 | tf_op jit(solution)/shard_map/feed_forward/pallas_call | solution.py:127
  258.7 12.4 %all-to-all-start = ((bf16[32,2,1152]{2,1,0:T(2,128)(2,1)}), bf16[32,2,1152]{2,1,0:T(2,128)(2,1)}, u32[]{:S(2)}, u32[]{:S(2)}) async-start(bf16[32,2,1152]{2,1,0:T(2,128)(2,1)} %broadcast_in_dim.12), calls=%async_computation | async-start | bytes 294912 | tf_op jit(solution)/shard_map/all_to_all | solution.py:1213
  274.2 5.5 all-to-all-done
  285.4 20.3 %feed_backward.2 = (f32[1024,1024]{1,0:T(8,128)}, f32[8,1024]{1,0:T(8,128)S(1)}, bf16[1024,1024]{1,0:T(8,128)(2,1)}, bf16[1024,1024]{1,0:T(8,128)(2,1)}, bf16[1024,1024]{1,0:T(8,128)(2,1)}) custom-call(s32[2]{0:T(128)S(1)} %copy-done.88, f32[16,1024]{1,0:T(8,128)S(1)} %copy-done.132, f32[1024,1024]{1,0:T(8,128)} %get-tuple-element.220.refs_4_.refs_2_, ...), custom_call_target="tpu_custom_call" | custom-call | flops 17600000000 | bytes 1048576 | tf_op jit(solution)/shard_map/feed_backward/pallas_call | solution.py:127
  308.0 12.2 %weights.3 = (bf16[8,64,1536]{2,1,0:T(8,128)(2,1)S(1)}, bf16[8,64,1536]{2,1,0:T(8,128)(2,1)S(1)}, bf16[8,64,1536]{2,1,0:T(8,128)(2,1)S(1)}, bf16[8,64,1536]{2,1,0:T(8,128)(2,1)S(1)}) custom-call(s32[2]{0:T(128)S(1)} %copy-done.88, bf16[1024,1024]{1,0:T(8,128)(2,1)S(1)} %copy-done.125, bf16[1024,1024]{1,0:T(8,128)(2,1)S(1)} %copy-done.126, ...), custom_call_target="tpu_custom_call" | custom-call | flops 9900000256 | bytes 1048576 | tf_op jit(solution)/shard_map/weights/pallas_call | solution.py:127
  324.6 20.5 %self_backward.2 = (bf16[512,3072]{1,0:T(8,128)(2,1)}, f32[1024,1024]{1,0:T(8,128)}, f32[8,1024]{1,0:T(8,128)}) custom-call(s32[2]{0:T(128)} %copy-done.85, f32[16,1024]{1,0:T(8,128)} %copy-done.129, f32[1024,1024]{1,0:T(8,128)} %get-tuple-element.214.refs_8_.refs_2_, f32[1024,1024]{1,0:T(8,128)} %get-tuple-element.230.refs_3_, ...), custom_call_target="tpu_custom_call" | custom-call | flops 22000001024 | bytes 1048576 | tf_op jit(solution)/shard_map/self_backward/pallas_call | solution.py:127
  352.9 20.8 %self_backward.3 = (bf16[512,3072]{1,0:T(8,128)(2,1)}, f32[1024,1024]{1,0:T(8,128)}, f32[8,1024]{1,0:T(8,128)}) custom-call(s32[2]{0:T(128)} %copy-done.85, f32[16,1024]{1,0:T(8,128)} %copy-done.129, f32[1024,1024]{1,0:T(8,128)} %get-tuple-element.214.refs_8_.refs_2_, f32[1024,1024]{1,0:T(8,128)} %get-tuple-element.230.refs_3_, ...), custom_call_target="tpu_custom_call", output_to_operand_aliasing={{1}: (22, {})} | custom-call | flops 22000001024 | bytes 1048576 | tf_op jit(solution)/shard_map/self_backward/pallas_call | solution.py:127
  380.8 10.9 %weights.4 = (bf16[8,64,1536]{2,1,0:T(8,128)(2,1)S(1)}, bf16[8,64,1536]{2,1,0:T(8,128)(2,1)}, bf16[8,64,1536]{2,1,0:T(8,128)(2,1)S(1)}, bf16[8,64,1536]{2,1,0:T(8,128)(2,1)S(1)}) custom-call(s32[2]{0:T(128)S(1)} %copy-done.90, bf16[1024,1024]{1,0:T(8,128)(2,1)S(1)} %copy-done.128, bf16[512,3072]{1,0:T(8,128)(2,1)S(1)} %copy-done.117, ...), custom_call_target="tpu_custom_call" | custom-call | flops 9900000256 | bytes 1048576 | tf_op jit(solution)/shard_map/weights/pallas_call | solution.py:127
  399.3 18.2 %feed_backward.3 = (f32[1024,1024]{1,0:T(8,128)}, f32[8,1024]{1,0:T(8,128)S(1)}, bf16[1024,1024]{1,0:T(8,128)(2,1)}, bf16[1024,1024]{1,0:T(8,128)(2,1)}, bf16[1024,1024]{1,0:T(8,128)(2,1)}) custom-call(s32[2]{0:T(128)S(1)} %copy-done.90, f32[16,1024]{1,0:T(8,128)S(1)} %copy-done.133, f32[1024,1024]{1,0:T(8,128)} %get-tuple-element.208.refs_8_.refs_2_, ...), custom_call_target="tpu_custom_call" | custom-call | flops 17600000000 | bytes 1048576 | tf_op jit(solution)/shard_map/feed_backward/pallas_call | solution.py:127
  436.0 12.1 %weights.5 = (bf16[8,64,1536]{2,1,0:T(8,128)(2,1)S(1)}, bf16[8,64,1536]{2,1,0:T(8,128)(2,1)S(1)}, bf16[8,64,1536]{2,1,0:T(8,128)(2,1)S(1)}, bf16[8,64,1536]{2,1,0:T(8,128)(2,1)S(1)}) custom-call(s32[2]{0:T(128)S(1)} %copy-done.90, bf16[1024,1024]{1,0:T(8,128)(2,1)S(1)} %copy-done.123, bf16[1024,1024]{1,0:T(8,128)(2,1)S(1)} %copy-done.101, ...), custom_call_target="tpu_custom_call" | custom-call | flops 9900000256 | bytes 1048576 | tf_op jit(solution)/shard_map/weights/pallas_call | solution.py:127
  455.3 24.4 %cross_backward.1 = (bf16[1024,1024]{1,0:T(8,128)(2,1)}, bf16[544,2048]{1,0:T(8,128)(2,1)}, bf16[8,64,640]{2,1,0:T(8,128)(2,1)S(1)}, bf16[8,64,640]{2,1,0:T(8,128)(2,1)S(1)}) custom-call(s32[2]{0:T(128)S(1)} %copy-done.90, f32[16,1024]{1,0:T(8,128)S(1)} %copy-done.134, f32[512,1024]{1,0:T(8,128)} %get-tuple-element.226.refs_2_, ...), custom_call_target="tpu_custom_call" | custom-call | flops 17600000000 | bytes 1048576 | tf_op jit(solution)/shard_map/cross_backward/pallas_call | solution.py:127
  486.4 5.2 collective-permute-done.76.refs_2_
  495.1 9.9 %last_weights.1 = (bf16[8,64,1024]{2,1,0:T(8,128)(2,1)S(1)}, bf16[8,64,1024]{2,1,0:T(8,128)(2,1)S(1)}, bf16[8,128,384]{2,1,0:T(8,128)(2,1)S(1)}, bf16[8,128,384]{2,1,0:T(8,128)(2,1)S(1)}) custom-call(s32[2]{0:T(128)S(1)} %copy-done.90, bf16[512,1024]{1,0:T(8,128)(2,1)S(1)} %copy-done.127, bf16[1024,1024]{1,0:T(8,128)(2,1)S(1)} %copy-done.103, ...), custom_call_target="tpu_custom_call" | custom-call | flops 6600000000 | bytes 1048576 | tf_op jit(solution)/shard_map/last_weights/pallas_call | solution.py:127
  512.1 13.6 %collective-permute-done.83.refs_2_ = bf16[8,32,1536]{2,1,0:T(8,128)(2,1)S(1)} collective-permute-done((bf16[8,32,1536]{2,1,0:T(8,128)(2,1)S(1)}, bf16[8,32,1536]{2,1,0:T(8,128)(2,1)S(1)}, u32[]{:S(2)}, u32[]{:S(2)}) %collective-permute-start.83) | collective-permute-done | bytes 786464 | tf_op jit(solution)/shard_map/ppermute | solution.py:1044
  537.5 5.7 collective-permute-done.88.refs_2_
  (624 shorter events, 270.3 us)
Async XLA Ops:
  49.4 26.2 %collective-permute-start.28 = (bf16[32,4096]{1,0:T(8,128)(2,1)S(1)}, bf16[32,4096]{1,0:T(8,128)(2,1)S(1)}, u32[]{:S(2)}, u32[]{:S(2)}) collective-permute-start(bf16[32,4096]{1,0:T(8,128)(2,1)S(1)} %get-tuple-element.201.refs_0_.refs_4_), channel_id=1, source_target_pairs={{0,16},{1,17},{2,18},{3,19},{4,20},{5,21},{6,22},{7,23},{8,24},{9,... | collective-permute-start | bytes 786440 | tf_op jit(solution)/shard_map/ppermute | solution.py:1044
  49.4 27.4 %collective-permute-start.27 = (bf16[32,4096]{1,0:T(8,128)(2,1)S(1)}, bf16[32,4096]{1,0:T(8,128)(2,1)S(1)}, u32[]{:S(2)}, u32[]{:S(2)}) collective-permute-start(bf16[32,4096]{1,0:T(8,128)(2,1)S(1)} %get-tuple-element.201.refs_0_.refs_4_), channel_id=1, source_target_pairs={{0,8},{1,9},{2,10},{3,11},{4,12},{5,13},{6,14},{7,15},{8,0},{9,1},... | collective-permute-start | bytes 786440 | tf_op jit(solution)/shard_map/ppermute | solution.py:1044
  51.1 26.2 %collective-permute-start.40 = (bf16[32,2048]{1,0:T(8,128)(2,1)S(1)}, bf16[32,2048]{1,0:T(8,128)(2,1)S(1)}, u32[]{:S(2)}, u32[]{:S(2)}) collective-permute-start(bf16[32,2048]{1,0:T(8,128)(2,1)S(1)} %get-tuple-element.209.refs_0_.refs_4_), channel_id=1, source_target_pairs={{0,24},{1,25},{2,26},{3,27},{4,28},{5,29},{6,30},{7,31},{8,16},{9,... | collective-permute-start | bytes 393224 | tf_op jit(solution)/shard_map/ppermute | solution.py:1044
  54.2 26.2 %collective-permute-start.39 = (bf16[32,2048]{1,0:T(8,128)(2,1)S(1)}, bf16[32,2048]{1,0:T(8,128)(2,1)S(1)}, u32[]{:S(2)}, u32[]{:S(2)}) collective-permute-start(bf16[32,2048]{1,0:T(8,128)(2,1)S(1)} %get-tuple-element.209.refs_0_.refs_4_), channel_id=1, source_target_pairs={{0,16},{1,17},{2,18},{3,19},{4,20},{5,21},{6,22},{7,23},{8,24},{9,... | collective-permute-start | bytes 393224 | tf_op jit(solution)/shard_map/ppermute | solution.py:1044
  58.2 29.9 %collective-permute-start.9 = (bf16[8,32,640]{2,1,0:T(8,128)(2,1)S(1)}, bf16[8,32,640]{2,1,0:T(8,128)(2,1)S(1)}, u32[]{:S(2)}, u32[]{:S(2)}) collective-permute-start(bf16[8,32,640]{2,1,0:T(8,128)(2,1)S(1)} %get-tuple-element.193.refs_9_.refs_2_), channel_id=1, source_target_pairs={{0,2},{1,3},{2,0},{3,1},{4,6},{5,7},{6,4},{7,5},{8,10},{9,11},{10,... | collective-permute-start | bytes 983048 | tf_op jit(solution)/shard_map/ppermute | solution.py:1044
  115.0 28.0 %collective-permute-start.37 = (bf16[4,32,2048]{2,1,0:T(8,128)(2,1)S(1)}, bf16[4,32,2048]{2,1,0:T(8,128)(2,1)S(1)}, u32[]{:S(2)}, u32[]{:S(2)}) collective-permute-start(bf16[4,32,2048]{2,1,0:T(8,128)(2,1)S(1)} %get-tuple-element.204.refs_5_.refs_2_), channel_id=1, source_target_pairs={{0,1},{1,0},{2,3},{3,2},{4,5},{5,4},{6,7},{7,6},{8,9},{9,8},{10,11... | collective-permute-start | bytes 1572872 | tf_op jit(solution)/shard_map/ppermute | solution.py:1044
  149.1 34.9 %collective-permute-start.41 = (bf16[8,32,2048]{2,1,0:T(8,128)(2,1)S(1)}, bf16[8,32,2048]{2,1,0:T(8,128)(2,1)}, u32[]{:S(2)}, u32[]{:S(2)}) collective-permute-start(bf16[8,32,2048]{2,1,0:T(8,128)(2,1)S(1)} %get-tuple-element.212.refs_11_.refs_3_.refs_7_.refs_6_.refs_10_), channel_id=1, source_target_pairs={{0,1},{1,0},{2,3},{3,2},{4,5},{5,4},{6,7},{7,6},{8,9},{9,8},{10,11... | collective-permute-start | bytes 3145736 | tf_op jit(solution)/shard_map/ppermute | solution.py:1044
  150.6 34.0 %collective-permute-start.44 = (bf16[8,32,2048]{2,1,0:T(8,128)(2,1)}, bf16[8,32,2048]{2,1,0:T(8,128)(2,1)}, u32[]{:S(2)}, u32[]{:S(2)}) collective-permute-start(bf16[8,32,2048]{2,1,0:T(8,128)(2,1)} %get-tuple-element.213.refs_12_.refs_11_.refs_15_.refs_14_.refs_18_), channel_id=1, source_target_pairs={{0,4},{1,5},{2,6},{3,7},{4,0},{5,1},{6,2},{7,3},{8,12},{9,13},{10,... | collective-permute-start | bytes 3145736 | tf_op jit(solution)/shard_map/ppermute | solution.py:1044
  202.5 31.0 %collective-permute-start.59 = (bf16[4,32,512]{2,1,0:T(8,128)(2,1)S(1)}, bf16[4,32,512]{2,1,0:T(8,128)(2,1)S(1)}, u32[]{:S(2)}, u32[]{:S(2)}) collective-permute-start(bf16[4,32,512]{2,1,0:T(8,128)(2,1)S(1)} %get-tuple-element.217.refs_5_.refs_2_), channel_id=1, source_target_pairs={{0,1},{1,0},{2,3},{3,2},{4,5},{5,4},{6,7},{7,6},{8,9},{9,8},{10,11... | collective-permute-start | bytes 393224 | tf_op jit(solution)/shard_map/ppermute | solution.py:1044
  203.0 35.3 %collective-permute-start.53 = (bf16[8,32,1024]{2,1,0:T(8,128)(2,1)S(1)}, bf16[8,32,1024]{2,1,0:T(8,128)(2,1)S(1)}, u32[]{:S(2)}, u32[]{:S(2)}) collective-permute-start(bf16[8,32,1024]{2,1,0:T(8,128)(2,1)S(1)} %get-tuple-element.218.refs_19_.refs_3_.refs_6_), channel_id=1, source_target_pairs={{0,2},{1,3},{2,0},{3,1},{4,6},{5,7},{6,4},{7,5},{8,10},{9,11},{10,... | collective-permute-start | bytes 1572872 | tf_op jit(solution)/shard_map/ppermute | solution.py:1044
  203.0 35.9 %collective-permute-start.56 = (bf16[8,32,1024]{2,1,0:T(8,128)(2,1)S(1)}, bf16[8,32,1024]{2,1,0:T(8,128)(2,1)S(1)}, u32[]{:S(2)}, u32[]{:S(2)}) collective-permute-start(bf16[8,32,1024]{2,1,0:T(8,128)(2,1)S(1)} %get-tuple-element.219.refs_20_.refs_7_.refs_10_), channel_id=1, source_target_pairs={{0,2},{1,3},{2,0},{3,1},{4,6},{5,7},{6,4},{7,5},{8,10},{9,11},{10,... | collective-permute-start | bytes 1572872 | tf_op jit(solution)/shard_map/ppermute | solution.py:1044
  203.5 35.4 %collective-permute-start.54 = (bf16[8,32,1024]{2,1,0:T(8,128)(2,1)S(1)}, bf16[8,32,1024]{2,1,0:T(8,128)(2,1)S(1)}, u32[]{:S(2)}, u32[]{:S(2)}) collective-permute-start(bf16[8,32,1024]{2,1,0:T(8,128)(2,1)S(1)} %collective-permute-done.52.refs_4_.refs_7_), channel_id=1, source_target_pairs={{0,2},{1,3},{2,0},{3,1},{4,6},{5,7},{6,4},{7,5},{8,10},{9,11},{10,... | collective-permute-start | bytes 1572872 | tf_op jit(solution)/shard_map/ppermute | solution.py:1044
  203.6 35.3 %collective-permute-start.57 = (bf16[8,32,1024]{2,1,0:T(8,128)(2,1)S(1)}, bf16[8,32,1024]{2,1,0:T(8,128)(2,1)S(1)}, u32[]{:S(2)}, u32[]{:S(2)}) collective-permute-start(bf16[8,32,1024]{2,1,0:T(8,128)(2,1)S(1)} %collective-permute-done.55.refs_8_.refs_11_), channel_id=1, source_target_pairs={{0,2},{1,3},{2,0},{3,1},{4,6},{5,7},{6,4},{7,5},{8,10},{9,11},{10,... | collective-permute-start | bytes 1572872 | tf_op jit(solution)/shard_map/ppermute | solution.py:1044
  236.7 34.9 %collective-permute-start.60 = (bf16[8,32,512]{2,1,0:T(8,128)(2,1)S(1)}, bf16[8,32,512]{2,1,0:T(8,128)(2,1)}, u32[]{:S(2)}, u32[]{:S(2)}) collective-permute-start(bf16[8,32,512]{2,1,0:T(8,128)(2,1)S(1)} %get-tuple-element.221.refs_11_.refs_2_), channel_id=1, source_target_pairs={{0,1},{1,0},{2,3},{3,2},{4,5},{5,4},{6,7},{7,6},{8,9},{9,8},{10,11... | collective-permute-start | bytes 786440 | tf_op jit(solution)/shard_map/ppermute | solution.py:1044
  238.3 33.5 %collective-permute-start.63 = (bf16[8,32,512]{2,1,0:T(8,128)(2,1)}, bf16[8,32,512]{2,1,0:T(8,128)(2,1)}, u32[]{:S(2)}, u32[]{:S(2)}) collective-permute-start(bf16[8,32,512]{2,1,0:T(8,128)(2,1)} %get-tuple-element.222.refs_12_.refs_6_), channel_id=1, source_target_pairs={{0,4},{1,5},{2,6},{3,7},{4,0},{5,1},{6,2},{7,3},{8,12},{9,13},{10,... | collective-permute-start | bytes 786440 | tf_op jit(solution)/shard_map/ppermute | solution.py:1044
  392.9 33.7 %collective-permute-start.72 = (bf16[8,64,1536]{2,1,0:T(8,128)(2,1)}, bf16[8,64,1536]{2,1,0:T(8,128)(2,1)S(1)}, u32[]{:S(2)}, u32[]{:S(2)}) collective-permute-start(bf16[8,64,1536]{2,1,0:T(8,128)(2,1)} %get-tuple-element.267), channel_id=1, source_target_pairs={{0,2},{1,3},{2,0},{3,1},{4,6},{5,7},{6,4},{7,5},{8,10},{9,11},{10,... | collective-permute-start | bytes 4718600 | tf_op jit(solution)/shard_map/ppermute | solution.py:1044
  392.9 33.7 %collective-permute-start.73 = (bf16[8,64,1536]{2,1,0:T(8,128)(2,1)S(1)}, bf16[8,64,1536]{2,1,0:T(8,128)(2,1)}, u32[]{:S(2)}, u32[]{:S(2)}) collective-permute-start(bf16[8,64,1536]{2,1,0:T(8,128)(2,1)S(1)} %get-tuple-element.269), channel_id=1, source_target_pairs={{0,2},{1,3},{2,0},{3,1},{4,6},{5,7},{6,4},{7,5},{8,10},{9,11},{10,... | collective-permute-start | bytes 4718600 | tf_op jit(solution)/shard_map/ppermute | solution.py:1044
  394.9 25.6 %collective-permute-start.109 = (bf16[32,1536]{1,0:T(8,128)(2,1)}, bf16[32,1536]{1,0:T(8,128)(2,1)}, u32[]{:S(2)}, u32[]{:S(2)}) collective-permute-start(bf16[32,1536]{1,0:T(8,128)(2,1)} %get-tuple-element.337), channel_id=1, source_target_pairs={{0,16},{1,17},{2,18},{3,19},{4,20},{5,21},{6,22},{7,23},{8,24},{9,... | collective-permute-start | bytes 294920 | tf_op jit(solution)/shard_map/ppermute | solution.py:1044
  395.9 25.6 %collective-permute-start.110 = (bf16[32,1536]{1,0:T(8,128)(2,1)}, bf16[32,1536]{1,0:T(8,128)(2,1)}, u32[]{:S(2)}, u32[]{:S(2)}) collective-permute-start(bf16[32,1536]{1,0:T(8,128)(2,1)} %get-tuple-element.338), channel_id=1, source_target_pairs={{0,24},{1,25},{2,26},{3,27},{4,28},{5,29},{6,30},{7,31},{8,16},{9,... | collective-permute-start | bytes 294920 | tf_op jit(solution)/shard_map/ppermute | solution.py:1044
  420.4 84.6 %collective-permute-start.111 = (bf16[32,1536]{1,0:T(8,128)(2,1)}, bf16[32,1536]{1,0:T(8,128)(2,1)}, u32[]{:S(2)}, u32[]{:S(2)}) collective-permute-start(bf16[32,1536]{1,0:T(8,128)(2,1)} %copy-done.78), channel_id=1, source_target_pairs={{0,8},{1,9},{2,10},{3,11},{4,12},{5,13},{6,14},{7,15},{8,0},{9,1},... | collective-permute-start | bytes 294920 | tf_op jit(solution)/shard_map/ppermute | solution.py:1044
  420.5 87.2 %collective-permute-start.112 = (bf16[32,1536]{1,0:T(8,128)(2,1)}, bf16[32,1536]{1,0:T(8,128)(2,1)}, u32[]{:S(2)}, u32[]{:S(2)}) collective-permute-start(bf16[32,1536]{1,0:T(8,128)(2,1)} %copy-done.77), channel_id=1, source_target_pairs={{0,16},{1,17},{2,18},{3,19},{4,20},{5,21},{6,22},{7,23},{8,24},{9,... | collective-permute-start | bytes 294920 | tf_op jit(solution)/shard_map/ppermute | solution.py:1044
  421.5 87.1 %collective-permute-start.113 = (bf16[32,1536]{1,0:T(8,128)(2,1)S(1)}, bf16[32,1536]{1,0:T(8,128)(2,1)}, u32[]{:S(2)}, u32[]{:S(2)}) collective-permute-start(bf16[32,1536]{1,0:T(8,128)(2,1)S(1)} %get-tuple-element.342), channel_id=1, source_target_pairs={{0,24},{1,25},{2,26},{3,27},{4,28},{5,29},{6,30},{7,31},{8,16},{9,... | collective-permute-start | bytes 294920 | tf_op jit(solution)/shard_map/ppermute | solution.py:1044
  452.3 28.2 %collective-permute-start.78 = (bf16[8,64,1536]{2,1,0:T(8,128)(2,1)S(1)}, bf16[8,64,1536]{2,1,0:T(8,128)(2,1)S(1)}, u32[]{:S(2)}, u32[]{:S(2)}) collective-permute-start(bf16[8,64,1536]{2,1,0:T(8,128)(2,1)S(1)} %get-tuple-element.287), channel_id=1, source_target_pairs={{0,2},{1,3},{2,0},{3,1},{4,6},{5,7},{6,4},{7,5},{8,10},{9,11},{10,... | collective-permute-start | bytes 4718600 | tf_op jit(solution)/shard_map/ppermute | solution.py:1044
  452.4 28.7 %collective-permute-start.79 = (bf16[8,64,1536]{2,1,0:T(8,128)(2,1)S(1)}, bf16[8,64,1536]{2,1,0:T(8,128)(2,1)S(1)}, u32[]{:S(2)}, u32[]{:S(2)}) collective-permute-start(bf16[8,64,1536]{2,1,0:T(8,128)(2,1)S(1)} %get-tuple-element.289), channel_id=1, source_target_pairs={{0,2},{1,3},{2,0},{3,1},{4,6},{5,7},{6,4},{7,5},{8,10},{9,11},{10,... | collective-permute-start | bytes 4718600 | tf_op jit(solution)/shard_map/ppermute | solution.py:1044
  (250 other events, 2786.0 us)
